TPU v7x, 32 devices: a whole 2x2x4 slice. The times are simulated.
32 devices in a mesh: pipe: 4 (over y, x), expert: 2 (over core), dp: 4 (over z).
Axes of the slice: x: 2, y: 2, z: 4, core: 2. Of those that a mesh axis runs over, the one named last changes fastest.
Arguments:
- hidden_in: bfloat16 [4096, 6144], P(('pipe', 'expert', 'dp'))
- norm_gain: float32 [4, 6144], P('pipe'), may hold values from 0.1 to 1.9
- w_gate: bfloat16 [4, 6144, 8192], P('pipe', None, ('expert', 'dp')), may hold values from -0.078125 to 0.078125
- w_up: bfloat16 [4, 6144, 8192], P('pipe', None, ('expert', 'dp')), may hold values from -0.078125 to 0.078125
- w_down: bfloat16 [4, 8192, 6144], P('pipe', ('expert', 'dp')), may hold values from -0.0625 to 0.0625
- expert_ids: int32 [4096, 2], P(('pipe', 'expert', 'dp')), may hold values from 0 to 7, as said below
- gate_weights: float32 [4096, 2], P(('pipe', 'expert', 'dp')), may hold values from 0.25 to 1
Outputs:
- passed_on: bfloat16 [4096, 6144], P(('pipe', 'expert', 'dp'))
Inputs may be any that keep to these rules, and one draw needn't show every extreme that they name: `expert_ids`: the two ids of a row differ. In every aligned block of 128 rows (the rows of one device) at most 64 rows name expert 0, and in each section's 8 blocks at least one block has 64 such rows; the 8 blocks of one section hold exactly 256 rows that name expert 0.
All inputs are finite; a program needn't handle non-finite values.
Results may differ from a plain program's by a relative error of at most 0.0045.
Values may be sent and summed in bfloat16 or wider, within the bound.
No kernel may reach another device: no remote copies, remote signals or barrier semaphores. Data moves between devices by JAX's collectives and lax.ppermute only.
A program may use at most 192 MiB of HBM per device.

v0:
```python
import jax
import jax.numpy as jnp
from jax import lax
from jax.sharding import PartitionSpec as P


def passed_along(block, axis, distance):
    devices = range(lax.axis_size(axis))
    route = [((i - distance) % len(devices), i) for i in devices]
    return lax.ppermute(block, axis, route)


def rms_scale(values_in, gain):
    values = values_in.astype(jnp.float32)
    mean_sq = jnp.mean(values * values, axis=-1, keepdims=True)
    return (values * lax.rsqrt(mean_sq + 1e-05) * gain).astype(jnp.bfloat16)


def expert_rows(normed, gate_matrix, up_matrix, down_matrix):
    gate = jnp.dot(normed, gate_matrix, preferred_element_type=jnp.float32)
    up_values = jnp.dot(normed, up_matrix, preferred_element_type=jnp.float32)
    hidden = (jax.nn.silu(gate) * up_values).astype(jnp.bfloat16)
    return jnp.dot(hidden, down_matrix, preferred_element_type=jnp.float32)


def per_device(hidden_in, norm_gain, w_gate, w_up, w_down, expert_ids, gate_weights):
    row_count = hidden_in.shape[0]
    capacity = row_count // 2
    normed = rms_scale(hidden_in, norm_gain[0])
    chosen = expert_ids == 0
    routed = jnp.any(chosen, axis=1)
    own_weight = jnp.sum(jnp.where(chosen, gate_weights, 0.0), axis=1)
    position = jnp.cumsum(routed.astype(jnp.int32)) - 1
    slot_grid = lax.broadcasted_iota(jnp.int32, (capacity, row_count), 0)
    token_grid = lax.broadcasted_iota(jnp.int32, (capacity, row_count), 1)
    picked = (position[None, :] == slot_grid) & routed[None, :]
    source = jnp.sum(jnp.where(picked, token_grid, 0), axis=1)
    filled = jnp.any(picked, axis=1)
    packed = jnp.where(
        filled[:, None], jnp.take(normed, source, axis=0), jnp.zeros_like(normed[:1])
    )
    gate_matrix = w_gate[0]
    up_matrix = w_up[0]
    down_matrix = w_down[0]
    terms = expert_rows(
        lax.all_gather(packed, ("expert", "dp"), axis=0, tiled=True),
        gate_matrix,
        up_matrix,
        down_matrix,
    )
    own_rows = lax.psum_scatter(
        terms.astype(jnp.bfloat16), ("expert", "dp"), scatter_dimension=0, tiled=True
    ).astype(jnp.float32)
    back = jnp.take(own_rows, jnp.clip(position, 0, capacity - 1), axis=0)
    branch = jnp.where(routed[:, None], back, 0.0)
    combined = (hidden_in.astype(jnp.float32) + own_weight[:, None] * branch).astype(jnp.bfloat16)
    return passed_along(combined, "pipe", 1)


def solution(mesh):
    return jax.shard_map(
        per_device,
        mesh=mesh,
        in_specs=(
            P(("pipe", "expert", "dp"), None),
            P("pipe", None),
            P("pipe", None, ("expert", "dp")),
            P("pipe", None, ("expert", "dp")),
            P("pipe", ("expert", "dp"), None),
            P(("pipe", "expert", "dp"), None),
            P(("pipe", "expert", "dp"), None),
        ),
        out_specs=P(("pipe", "expert", "dp"), None),
        check_vma=False,
    )
```

profile of v0, /device:TPU:0, one launch (start us, length us, event | category | flops | bytes accessed | tf_op | source)
XLA Modules:
  0.0 291.0 jit_solution(1206754820473103689)
XLA Ops:
  6.5 0.7 fusion.19
  7.2 0.1 copy.10
  7.4 0.2 reduce-window.4
  7.5 0.1 fusion.15
  7.6 0.1 select_reduce_fusion
  7.8 0.1 fusion.17
  7.9 1.8 fusion.9
  9.7 1.9 fusion.11
  11.6 1.0 gather_fusion
  12.6 1.0 select_select_fusion
  13.7 0.0 all-gather.2.cloned.1.call-update
  13.7 0.0 reduce-scatter.2.cloned.1.call-start
  13.7 67.6 %all-gather.2.cloned.1.call-done = bf16[512,6144]{1,0:T(8,128)(2,1)} async-done(((bf16[64,6144]{1,0:T(8,128)(2,1)}), bf16[512,6144]{1,0:T(8,128)(2,1)}) %all-gather.2.cloned.1.call-update) | async-done | bytes 6291472 | tf_op jit(solution)/shard_map/all_gather | solution.py:46
  81.3 11.6 %fusion.2 = f32[512,1024]{1,0:T(8,128)S(1)} fusion(bf16[512,6144]{1,0:T(8,128)(2,1)} %all-gather.2.cloned.1.call-done, bf16[1,6144,1024]{2,1,0:T(8,128)(2,1)} %param.10), kind=kOutput, calls=%fused_computation.4 | convolution fusion | flops 6442450944 | bytes 20971520 | tf_op jit(solution)/shard_map/dot_general | solution.py:21
  92.9 10.1 %multiply_convert_fusion = bf16[512,1024]{1,0:T(8,128)(2,1)S(1)} fusion(f32[512,1024]{1,0:T(8,128)S(1)} %fusion.2, bf16[512,6144]{1,0:T(8,128)(2,1)S(1)} %copy-done.3, bf16[1,6144,1024]{2,1,0:T(8,128)(2,1)} %param.9), kind=kOutput, calls=%fused_computation.16 | convolution fusion | flops 6445596672 | bytes 22020096 | tf_op jit(solution)/shard_map/dot_general | solution.py:20
  103.0 8.6 %fusion.6 = bf16[512,6144]{1,0:T(8,128)(2,1)} fusion(bf16[512,1024]{1,0:T(8,128)(2,1)S(1)} %multiply_convert_fusion, bf16[1,1024,6144]{2,1,0:T(8,128)(2,1)S(1)} %bitcast.25), kind=kOutput, calls=%fused_computation.8 | convolution fusion | flops 6445596672 | bytes 19922944 | tf_op jit(solution)/shard_map/dot_general | solution.py:23
  111.7 0.6 copy-done.1
  112.4 126.0 %reduce-scatter.2.cloned.1.call-done = bf16[64,6144]{1,0:T(8,128)(2,1)} async-done(((bf16[512,6144]{1,0:T(8,128)(2,1)}), bf16[64,6144]{1,0:T(8,128)(2,1)}) %reduce-scatter.2.cloned.1.call-update) | async-done | bytes 786448 | tf_op jit(solution)/shard_map/reduce_scatter | solution.py:51
  238.3 1.2 convert_element_type.38
  239.6 3.2 %gather_fusion.1 = f32[128,6144]{1,0:T(8,128)} fusion(f32[64,6144]{1,0:T(8,128)S(1)} %convert_element_type.38, s32[1024]{0:T(1024)S(1)} %pad_clamp_fusion), kind=kCustom, calls=%fused_computation.1 | custom fusion | bytes 6291968 | tf_op jit(solution)/shard_map/jit(_take)/gather | solution.py:54
  242.8 2.7 fusion.12
  245.5 1.5 collective-permute-start
  247.0 36.0 %collective-permute-done = bf16[128,6144]{1,0:T(8,128)(2,1)S(1)} collective-permute-done((bf16[128,6144]{1,0:T(8,128)(2,1)S(1)}, bf16[128,6144]{1,0:T(8,128)(2,1)S(1)}, u32[]{:S(2)}, u32[]{:S(2)}) %collective-permute-start) | collective-permute-done | bytes 1572896 | tf_op jit(solution)/shard_map/ppermute | solution.py:10
  283.0 1.1 copy.12
  (24 shorter events, 0.1 us)
Async XLA Ops:
  6.5 74.8 %all-gather.2.cloned.1.call-start = ((), (), s32[]{:S(2)}) async-start(), calls=%async_computation.1 | async-start | bytes 7077888 | tf_op jit(solution)/shard_map/all_gather | solution.py:46
  13.7 224.7 %reduce-scatter.2.cloned.1.call-start = ((), (), s32[]{:S(2)}) async-start(), calls=%async_computation.2 | async-start | bytes 7077888 | tf_op jit(solution)/shard_map/reduce_scatter | solution.py:51
  81.3 11.6 %copy-start.3 = (bf16[512,6144]{1,0:T(8,128)(2,1)S(1)}, bf16[512,6144]{1,0:T(8,128)(2,1)}, u32[]{:S(2)}) copy-start(bf16[512,6144]{1,0:T(8,128)(2,1)} %all-gather.2.cloned.1.call-done) | copy-start | bytes 18874372
  81.3 21.7 %slice-start = ((s8[12582912]{0:T(1024)(128)(4,1)}), s8[4194304]{0:T(1024)(128)(4,1)S(1)}, s32[]{:S(2)}) async-start(s8[12582912]{0:T(1024)(128)(4,1)} %bitcast.24), calls=%async_computation.3 | async-start | bytes 8388608
  81.3 21.7 %slice-start.1 = ((s8[12582912]{0:T(1024)(128)(4,1)}), s8[4194304]{0:T(1024)(128)(4,1)S(1)}, s32[]{:S(2)}) async-start(s8[12582912]{0:T(1024)(128)(4,1)} %bitcast.24), calls=%async_computation.4 | async-start | bytes 8388608
  92.9 10.1 %slice-start.2 = ((s8[12582912]{0:T(1024)(128)(4,1)}), s8[4194304]{0:T(1024)(128)(4,1)S(1)}, s32[]{:S(2)}) async-start(s8[12582912]{0:T(1024)(128)(4,1)} %bitcast.24), calls=%async_computation.5 | async-start | bytes 8388608
  111.6 0.7 copy-start.1
  111.6 0.7 copy-start.2
  239.6 3.2 %copy-start = (bf16[128,6144]{1,0:T(8,128)(2,1)S(1)}, bf16[128,6144]{1,0:T(8,128)(2,1)}, u32[]{:S(2)}) copy-start(bf16[128,6144]{1,0:T(8,128)(2,1)} %param.7) | copy-start | bytes 4718596
  245.5 37.5 %collective-permute-start = (bf16[128,6144]{1,0:T(8,128)(2,1)S(1)}, bf16[128,6144]{1,0:T(8,128)(2,1)S(1)}, u32[]{:S(2)}, u32[]{:S(2)}) collective-permute-start(bf16[128,6144]{1,0:T(8,128)(2,1)S(1)} %fusion.12), channel_id=1, source_target_pairs={{24,0},{0,8},{8,16},{16,24},{25,1},{1,9},{9,17},{17,25},{26,2},{2,... | collective-permute-start | bytes 4718600 | tf_op jit(solution)/shard_map/ppermute | solution.py:10
Sparse Core Ops, SparseCore 0:
  13.8 67.4 all-gather.1
  111.8 126.5 reduce-scatter.1
where the time goes:
time: 291 us
  waiting for transfers between devices  230 us (79%)
  matrix products  30.3 us (10%)
  between operations  13.5 us (5%)
  other arithmetic  9.89 us (3%)
  local copies, waits for them, and re-layouts  6.13 us (2%)
    reduce_scatter x1, waiting for transfers between devices, per_device(): lax.psum_scatter(terms.astype(jnp.bfloat16), ('expert', 'dp'), scatter_di...  126 us
    all_gather x1, waiting for transfers between devices, per_device(): lax.all_gather(packed, ('expert', 'dp'), axis=0, tiled=True)  67.6 us
    ppermute x1, waiting for transfers between devices, passed_along(): return lax.ppermute(block, axis, route)  36 us
    dot_general x1, matrix products, expert_rows(): up_values = jnp.dot(normed, up_matrix, preferred_element_type=jnp.float32)  11.6 us
    dot_general x1, matrix products, expert_rows(): gate = jnp.dot(normed, gate_matrix, preferred_element_type=jnp.float32)  10.1 us
    dot_general x1, matrix products, expert_rows(): return jnp.dot(hidden, down_matrix, preferred_element_type=jnp.float32)  8.58 us
  transfers between devices with their start and end apart: 3, of which 3 were waited for; matrix products, arithmetic and copies ran while one was open for 0% of the time, Pallas kernels for 0%

commit v1 on v0

--- a/solution.py
+++ b/solution.py
@@ -1,13 +1,330 @@
+import functools
+
 import jax
 import jax.numpy as jnp
 from jax import lax
+from jax.experimental import pallas as pl
+from jax.experimental.pallas import tpu as pltpu
 from jax.sharding import PartitionSpec as P
 
-
-def passed_along(block, axis, distance):
-    devices = range(lax.axis_size(axis))
-    route = [((i - distance) % len(devices), i) for i in devices]
-    return lax.ppermute(block, axis, route)
+MIB = 2**20
+VMEM_HIDDEN = 34
+VMEM_DOWN = 24
+PIECES = 4
+
+
+def next_section(block):
+    count = lax.axis_size("pipe")
+    return lax.ppermute(block, "pipe", [(i, (i + 1) % count) for i in range(count)])
+
+
+def other_core(block):
+    count = lax.axis_size("expert")
+    return lax.ppermute(block, "expert", [(i, (i + 1) % count) for i in range(count)])
+
+
+def routing_rows(ids, weights):
+    rows = ids.shape[1]
+    chosen = ids == 0
+    routed = jnp.max(jnp.where(chosen, 1.0, 0.0), axis=0, keepdims=True)
+    own = jnp.sum(jnp.where(chosen, weights, 0.0), axis=0, keepdims=True)
+    before = lax.broadcasted_iota(jnp.int32, (rows, rows), 0)
+    after = lax.broadcasted_iota(jnp.int32, (rows, rows), 1)
+    upper = jnp.where(before <= after, 1.0, 0.0).astype(jnp.bfloat16)
+    counted = jnp.dot(
+        jnp.broadcast_to(routed, (16, rows)).astype(jnp.bfloat16), upper, preferred_element_type=jnp.float32
+    )[0:1]
+    place = jnp.where(routed > 0.5, counted - 1.0, -1.0)
+    return place, own
+
+
+def as_column(row):
+    size = row.shape[1]
+    on_row = lax.broadcasted_iota(jnp.int32, (size, size), 0)
+    on_col = lax.broadcasted_iota(jnp.int32, (size, size), 1)
+    return jnp.sum(jnp.where(on_row == on_col, row, 0.0), axis=1, keepdims=True)
+
+
+def pack_kernel(step, sizes, x_hbm, gain_hbm, ids_hbm, weights_hbm, meta_ref, *refs):
+    packed, (values, x_ref, gain_ref, ids_ref, weights_ref, sem) = refs[: len(sizes)], refs[len(sizes) :]
+    copies = [
+        pltpu.make_async_copy(source, target, sem.at[i])
+        for i, (source, target) in enumerate(
+            [(ids_hbm, ids_ref), (weights_hbm, weights_ref), (gain_hbm, gain_ref), (x_hbm, x_ref)]
+        )
+    ]
+    for copy in copies:
+        copy.start()
+    for copy in copies[:2]:
+        copy.wait()
+    rows, width = x_ref.shape
+    slots = values.shape[0]
+    place, own = routing_rows(ids_ref[...], weights_ref[...])
+    meta_ref[0:1] = place
+    meta_ref[1:2] = own
+    slot = lax.broadcasted_iota(jnp.int32, (slots, rows), 0).astype(jnp.float32)
+    picked = jnp.where(slot == place, 1.0, 0.0).astype(jnp.bfloat16)
+    for copy in copies[2:]:
+        copy.wait()
+    total = jnp.zeros((slots, 1), jnp.float32)
+    for start in range(0, width, step):
+        part = jnp.dot(picked, x_ref[:, start : start + step], preferred_element_type=jnp.float32)
+        values[:, start : start + step] = part
+        total += jnp.sum(part * part, axis=1, keepdims=True)
+    scale = lax.rsqrt(total / width + 1e-05)
+    for start in range(0, width, step):
+        normed = values[:, start : start + step] * scale * gain_ref[:, start : start + step]
+        normed = normed.astype(jnp.bfloat16)
+        first = 0
+        for size, out in zip(sizes, packed):
+            out[:, start : start + step] = normed[first : first + size]
+            first += size
+
+
+def pack(x, gain, ids, weights, sizes):
+    rows, width = x.shape
+    slots = sum(sizes)
+    vmem = pl.BlockSpec(memory_space=pltpu.VMEM)
+    stays = pl.BlockSpec(memory_space=pltpu.HBM)
+    return pl.pallas_call(
+        functools.partial(pack_kernel, 512, sizes),
+        out_shape=[jax.ShapeDtypeStruct((2, rows), jnp.float32)]
+        + [jax.ShapeDtypeStruct((size, width), jnp.bfloat16) for size in sizes],
+        in_specs=[stays] * 4,
+        out_specs=[vmem] * (len(sizes) + 1),
+        scratch_shapes=[
+            pltpu.VMEM((slots, width), jnp.float32),
+            pltpu.VMEM(x.shape, x.dtype),
+            pltpu.VMEM(gain.shape, gain.dtype),
+            pltpu.VMEM(ids.shape, ids.dtype),
+            pltpu.VMEM(weights.shape, weights.dtype),
+            pltpu.SemaphoreType.DMA((4,)),
+        ],
+        compiler_params=pltpu.CompilerParams(vmem_limit_bytes=8 * MIB),
+        cost_estimate=pl.CostEstimate(flops=2 * slots * rows * width, bytes_accessed=3 * rows * width, transcendentals=slots),
+        name="pack_rows",
+    )(*(pltpu.with_memory_space_constraint(each, pltpu.HBM) for each in (x, gain, ids, weights)))
+
+
+def combine_kernel(step, sizes, pieces, meta_ref, *refs):
+    inputs, refs = refs[:pieces], refs[pieces:]
+    arrived, (out, sums) = refs[:-2], refs[-2:]
+    rows, width = out.shape
+    each = rows // pieces
+    first = 0
+    for k, size in enumerate(sizes):
+        total = sum(part[...].astype(jnp.float32) for part in arrived[3 * k : 3 * k + 3])
+        sums[first : first + size] = total.astype(jnp.bfloat16)
+        first += size
+    place, own = as_column(meta_ref[0:1]), as_column(meta_ref[1:2])
+    slot = lax.broadcasted_iota(jnp.int32, (rows, first), 1).astype(jnp.float32)
+    spread = jnp.where(slot == place, 1.0, 0.0).astype(jnp.bfloat16)
+    for start in range(0, width, step):
+        branch = own * jnp.dot(spread, sums[:, start : start + step], preferred_element_type=jnp.float32)
+        for p, piece in enumerate(inputs):
+            mine = slice(p * each, (p + 1) * each)
+            x = piece[:, start : start + step].astype(jnp.float32)
+            out[mine, start : start + step] = (x + branch[mine]).astype(jnp.bfloat16)
+
+
+def combine(inputs, meta, arrived):
+    rows, width = meta.shape[1], inputs[0].shape[1]
+    sizes = [part.shape[0] for part in arrived[::3]]
+    vmem = pl.BlockSpec(memory_space=pltpu.VMEM)
+    return pl.pallas_call(
+        functools.partial(combine_kernel, 512, sizes, len(inputs)),
+        out_shape=jax.ShapeDtypeStruct((rows, width), jnp.bfloat16),
+        in_specs=[vmem] * (1 + len(inputs) + len(arrived)),
+        out_specs=vmem,
+        scratch_shapes=[pltpu.VMEM((sum(sizes), width), jnp.bfloat16)],
+        compiler_params=pltpu.CompilerParams(vmem_limit_bytes=8 * MIB),
+        cost_estimate=pl.CostEstimate(flops=rows * rows * width, bytes_accessed=5 * rows * width, transcendentals=0),
+        name="combine_rows",
+    )(meta, *inputs, *arrived)
+
+
+def hidden_kernel(cols, parts, *refs):
+    blocks, (gate_m, up_m, out, x_v, wide_v, wide_sem) = refs[:8], refs[8:]
+    rows = blocks[0].shape[0]
+    tiles = gate_m.shape[1] // cols
+
+    depth = x_v.shape[1] // parts
+
+    def pair_copies(t, slot, part):
+        at, rows_at = pl.ds(t * cols, cols), pl.ds(part * depth, depth)
+        return [
+            pltpu.make_async_copy(gate_m.at[rows_at, at], wide_v.at[slot, rows_at, pl.ds(0, cols)], wide_sem.at[slot, part, 0]),
+            pltpu.make_async_copy(up_m.at[rows_at, at], wide_v.at[slot, rows_at, pl.ds(cols, cols)], wide_sem.at[slot, part, 1]),
+        ]
+
+    for t in range(tiles):
+        for part in range(parts):
+            for copy in pair_copies(t, t, part):
+                copy.start()
+    for i, block in enumerate(blocks):
+        x_v[i * rows : (i + 1) * rows] = block[...]
+
+    for t in range(tiles):
+        for part in range(parts):
+            for copy in pair_copies(t, t, part):
+                copy.wait()
+            if t == 0:
+                k = slice(part * depth, (part + 1) * depth)
+                piece = jnp.dot(x_v[:, k], wide_v[t, k], preferred_element_type=jnp.float32)
+                both = piece if part == 0 else both + piece
+        if t > 0:
+            both = jnp.dot(x_v[...], wide_v[t], preferred_element_type=jnp.float32)
+        gate, up = both[:, :cols], both[:, cols:]
+        out[:, t * cols : (t + 1) * cols] = (gate / (1.0 + jnp.exp(-gate)) * up).astype(jnp.bfloat16)
+
+
+def down_kernel(cols, hidden, down_m, *refs):
+    outs, (down_v, down_sem) = refs[:4], refs[4:]
+    width = down_m.shape[1]
+    tiles, slots = width // cols, down_v.shape[0]
+
+    def down_copy(t, slot):
+        return pltpu.make_async_copy(down_m.at[:, pl.ds(t * cols, cols)], down_v.at[slot], down_sem.at[slot])
+
+    for t in range(slots):
+        down_copy(t, t).start()
+    for t in range(tiles):
+        slot = t % slots
+        down_copy(t, slot).wait()
+        total = jnp.dot(hidden[...], down_v[slot], preferred_element_type=jnp.float32).astype(jnp.bfloat16)
+        first = 0
+        for out in outs:
+            out[:, t * cols : (t + 1) * cols] = total[first : first + out.shape[0]]
+            first += out.shape[0]
+        if t + slots < tiles:
+            down_copy(t + slots, slot).start()
+
+
+def in_hbm(matrix):
+    return pltpu.with_memory_space_constraint(matrix, pltpu.HBM)
+
+
+def expert_hidden(blocks, gate_m, up_m):
+    rows, width = blocks[0].shape
+    hidden = gate_m.shape[1]
+    cols, parts = 256, 4
+    vmem, stays = pl.BlockSpec(memory_space=pltpu.VMEM), pl.BlockSpec(memory_space=pltpu.HBM)
+    return pl.pallas_call(
+        functools.partial(hidden_kernel, cols, parts),
+        out_shape=jax.ShapeDtypeStruct((8 * rows, hidden), jnp.bfloat16),
+        in_specs=[vmem] * 8 + [stays] * 2,
+        out_specs=vmem,
+        scratch_shapes=[
+            pltpu.VMEM((8 * rows, width), jnp.bfloat16),
+            pltpu.VMEM((hidden // cols, width, 2 * cols), jnp.bfloat16),
+            pltpu.SemaphoreType.DMA((hidden // cols, parts, 2)),
+        ],
+        compiler_params=pltpu.CompilerParams(vmem_limit_bytes=VMEM_HIDDEN * MIB),
+        cost_estimate=pl.CostEstimate(
+            flops=32 * rows * width * hidden,
+            bytes_accessed=4 * width * hidden + 16 * rows * width,
+            transcendentals=8 * rows * hidden,
+        ),
+        name="expert_hidden",
+    )(*blocks, in_hbm(gate_m), in_hbm(up_m))
+
+
+def expert_down(hidden, down_m):
+    rows, width = hidden.shape[0] // 8, down_m.shape[1]
+    cols = 1024
+    vmem, stays = pl.BlockSpec(memory_space=pltpu.VMEM), pl.BlockSpec(memory_space=pltpu.HBM)
+    first, rest = [jax.ShapeDtypeStruct((count * rows, width), jnp.bfloat16) for count in (1, 3)]
+    return pl.pallas_call(
+        functools.partial(down_kernel, cols),
+        out_shape=[first, rest, first, rest],
+        in_specs=[vmem, stays],
+        out_specs=[vmem] * 4,
+        scratch_shapes=[
+            pltpu.VMEM((width // cols, down_m.shape[0], cols), jnp.bfloat16),
+            pltpu.SemaphoreType.DMA((width // cols,)),
+        ],
+        compiler_params=pltpu.CompilerParams(vmem_limit_bytes=VMEM_DOWN * MIB),
+        cost_estimate=pl.CostEstimate(
+            flops=16 * rows * width * down_m.shape[0],
+            bytes_accessed=2 * width * down_m.shape[0] + 32 * rows * width,
+            transcendentals=0,
+        ),
+        name="expert_down",
+    )(hidden, in_hbm(down_m))
+
+
+def add(*terms):
+    total = terms[0].astype(jnp.float32)
+    for term in terms[1:]:
+        total += term.astype(jnp.float32)
+    return total.astype(jnp.bfloat16)
+
+
+def after(block, *earlier):
+    return lax.optimization_barrier((block, *earlier))[0]
+
+
+def route(block, target, cores=(0, 1)):
+    sections, chips = lax.axis_size("pipe"), lax.axis_size("dp")
+    index = lambda section, core, chip: ((section % sections) * 2 + core) * chips + chip
+    pairs = [
+        (index(section, core, chip), index(*target(section, core, chip)))
+        for section in range(sections)
+        for core in cores
+        for chip in range(chips)
+    ]
+    return lax.ppermute(block, ("pipe", "expert", "dp"), pairs)
+
+
+def chip(mask):
+    return lambda s, c, z: (s, c, z ^ mask)
+
+
+def next_chip(mask):
+    return lambda s, c, z: (s + 1, c, z ^ mask)
+
+
+def per_device(hidden_in, norm_gain, w_gate, w_up, w_down, expert_ids, gate_weights):
+    rows = hidden_in.shape[0]
+    size, each = rows // 4, rows // PIECES
+    meta, *packed = pack(hidden_in, norm_gain, expert_ids.T, gate_weights.T, [size, size // 2, size // 2])
+    meta_before = next_section(meta)
+    halves = [packed[0], jnp.concatenate(packed[1:], axis=0)]
+    swapped = other_core(packed[0])
+    early = after(hidden_in, swapped)
+    inputs = [next_section(early[p * each : (p + 1) * each]) for p in range(PIECES)]
+
+    def expert_hidden_of(blocks, theirs):
+        return expert_hidden(blocks + theirs, w_gate[0], w_up[0])
+
+    def scatter(terms, wait_for_own):
+        keep_first, keep_rest, send_first, send_rest = terms
+        partner = route(add(keep_first, other_core(send_first)), chip(1))
+        rest = add(keep_rest, other_core(send_rest))
+        stays = route(rest[2 * size :], next_chip(0))
+        across = route(rest[size : 2 * size], next_chip(1))
+        if wait_for_own:
+            partner = after(partner, stays)
+        return [stays, across, route(add(rest[:size], partner), next_chip(3))]
+
+    cross, near = route(packed[0], chip(3)), route(after(packed[0], swapped), chip(1))
+    far = route(after(cross, *inputs[:2]), chip(1))
+    cross_swapped = other_core(cross)
+    cross_next = [route(after(block, cross_swapped), chip(3)) for block in packed[1:]]
+    near_next = route(after(halves[1], cross_swapped), chip(1))
+    mine = [far, cross, near, after(packed[0], inputs[2], cross_next[0], meta_before)]
+    hidden = expert_hidden_of(mine, [other_core(far), cross_swapped, other_core(near), swapped])
+    cross_next = jnp.concatenate([after(block, hidden) for block in cross_next], axis=0)
+    far_next = route(after(cross_next, hidden), chip(1))
+    terms = expert_down(after(hidden, near_next, inputs[3]), w_down[0])
+    arrived = scatter([after(term, far_next) for term in terms], True)
+
+    mine = [far_next, cross_next, near_next, halves[1]]
+    hidden = expert_hidden_of(mine, [other_core(block) for block in mine])
+    keep_first, keep_rest, send_first, send_rest = expert_down(hidden, w_down[0])
+    send_first, send_rest = after(send_first, *arrived), after(send_rest, *arrived)
+    arrived += scatter([keep_first, keep_rest, send_first, send_rest], False)
+    return combine(inputs, meta_before, arrived)
 
 
 def rms_scale(values_in, gain):
@@ -23,7 +340,7 @@
     return jnp.dot(hidden, down_matrix, preferred_element_type=jnp.float32)
 
 
-def per_device(hidden_in, norm_gain, w_gate, w_up, w_down, expert_ids, gate_weights):
+def per_device_any(hidden_in, norm_gain, w_gate, w_up, w_down, expert_ids, gate_weights):
     row_count = hidden_in.shape[0]
     capacity = row_count // 2
     normed = rms_scale(hidden_in, norm_gain[0])
@@ -54,12 +371,13 @@
     back = jnp.take(own_rows, jnp.clip(position, 0, capacity - 1), axis=0)
     branch = jnp.where(routed[:, None], back, 0.0)
     combined = (hidden_in.astype(jnp.float32) + own_weight[:, None] * branch).astype(jnp.bfloat16)
-    return passed_along(combined, "pipe", 1)
+    return next_section(combined)
 
 
 def solution(mesh):
+    paired = mesh.shape["dp"] == 4 and mesh.shape["expert"] == 2
     return jax.shard_map(
-        per_device,
+        per_device if paired else per_device_any,
         mesh=mesh,
         in_specs=(
             P(("pipe", "expert", "dp"), None),

time: 291 us -> 146 us (0.50)
  waiting for transfers between devices: 230 us -> 72.3 us
  Pallas kernels: 0 us -> 37.3 us
  starting transfers between devices: 1.57 us -> 33.9 us
  matrix products: 30.3 us -> 0 us
  between operations: 13.5 us -> 0.2 us
  other arithmetic: 9.89 us -> 0.99 us
  local copies, waits for them, and re-layouts: 6.13 us -> 0.29 us
    reduce_scatter x1 -> x0, waiting for transfers between devices: 126 us -> none  [per_device(): lax.psum_scatter(terms.astype(jnp.bfloat16), ('expert', 'dp'), scatter_di...]
    all_gather x1 -> x0, waiting for transfers between devices: 67.6 us -> none  [per_device(): lax.all_gather(packed, ('expert', 'dp'), axis=0, tiled=True)]
    pallas_call x0 -> x6, Pallas kernels: none -> 37.3 us  [the longest x2 21.3 us: expert_hidden(): pl.pallas_call(functools.partial(hidden_kernel, cols, parts), out_shape=j...]
    ppermute x1 -> x32, waiting for transfers between devices: 36 us -> 72.3 us  [the longest x15 57.9 us: route(): return lax.ppermute(block, ('pipe', 'expert', 'dp'), pairs)]
    ppermute x1 -> x32, starting transfers between devices: 1.52 us -> 33.9 us  [the longest x15 26 us: route(): return lax.ppermute(block, ('pipe', 'expert', 'dp'), pairs)]
    dot_general x3 -> x0, matrix products: 30.3 us -> none  [the longest x1 11.6 us: expert_rows(): up_values = jnp.dot(normed, up_matrix, preferred_element_type=jnp.float32)]
    convert_element_type x4 -> x6, other arithmetic: 5.8 us -> 0.99 us  [add(): return total.astype(jnp.bfloat16)]
    gather x2 -> x0, local copies, waits for them, and re-layouts: 4.19 us -> none  [the longest x1 3.18 us: per_device(): back = jnp.take(own_rows, jnp.clip(position, 0, capacity - 1), axis=0)]
  transfers between devices with their start and end apart: 3 -> 32, of which waited for: 3 -> 17; matrix products, arithmetic and copies ran while one was open for 0% -> 1% of each run, Pallas kernels for 0% -> 23%
where the time goes in v1:
time: 146 us; the launch traced here: 145 us
  waiting for transfers between devices  72.3 us (50%)
  Pallas kernels  37.3 us (26%)
  starting transfers between devices  33.9 us (23%)
    ppermute x15, waiting for transfers between devices, route(): return lax.ppermute(block, ('pipe', 'expert', 'dp'), pairs)  57.9 us
    ppermute x15, starting transfers between devices, route(): return lax.ppermute(block, ('pipe', 'expert', 'dp'), pairs)  26 us
    pallas_call x2, Pallas kernels, expert_hidden(): pl.pallas_call(functools.partial(hidden_kernel, cols, parts), out_shape=j...  21.3 us
    pallas_call x2, Pallas kernels, expert_down(): pl.pallas_call(functools.partial(down_kernel, cols), out_shape=[first, re...  11.8 us
    ppermute x5, waiting for transfers between devices, next_section(): lax.ppermute(block, 'pipe', [(i, (i + 1) % count) for i in range(count)])  10.7 us
    ppermute x5, starting transfers between devices, next_section(): lax.ppermute(block, 'pipe', [(i, (i + 1) % count) for i in range(count)])  5.83 us
    ppermute x12, waiting for transfers between devices, other_core(): lax.ppermute(block, 'expert', [(i, (i + 1) % count) for i in range(count)])  3.69 us
  transfers between devices with their start and end apart: 32, of which 17 were waited for; matrix products, arithmetic and copies ran while one was open for 1% of the time, Pallas kernels for 23%

profile of v1, /device:TPU:0, one launch (start us, length us, event | category | flops | bytes accessed | tf_op | source)
XLA Modules:
  0.0 145.0 jit_solution(10605348473376532869)
XLA Ops:
  0.0 2.2 %pack_rows.1 = (f32[2,128]{1,0:T(2,128)S(1)}, bf16[32,6144]{1,0:T(8,128)(2,1)S(1)}, bf16[16,6144]{1,0:T(8,128)(2,1)S(1)}, bf16[16,6144]{1,0:T(8,128)(2,1)S(1)}) custom-call(bf16[128,6144]{1,0:T(8,128)(2,1)} %x_hbm.1, f32[1,6144]{1,0:T(1,128)} %gain_hbm.1, s32[2,128]{1,0:T(2,128)} %bitcast.11, f32[2,128]{1,0:T(2,128)} %bitcast.12), custom_call_target="tpu_custom_call" | custom-call | flops 100663296 | bytes 2359296 | tf_op jit(solution)/shard_map/pack_rows/pallas_call | solution.py:89
  2.7 4.7 %collective-permute-start.6 = (bf16[32,6144]{1,0:T(8,128)(2,1)S(1)}, bf16[32,6144]{1,0:T(8,128)(2,1)S(1)}, u32[]{:S(2)}, u32[]{:S(2)}) collective-permute-start(bf16[32,6144]{1,0:T(8,128)(2,1)S(1)} %get-tuple-element.42.refs_3_), channel_id=1, source_target_pairs={{0,3},{1,2},{2,1},{3,0},{4,7},{5,6},{6,5},{7,4},{8,11},{9,10},{10,... | collective-permute-start | bytes 1179656 | tf_op jit(solution)/shard_map/ppermute | solution.py:276
  12.1 5.4 %collective-permute-done.6.refs_1_ = bf16[32,6144]{1,0:T(8,128)(2,1)S(1)} collective-permute-done((bf16[32,6144]{1,0:T(8,128)(2,1)S(1)}, bf16[32,6144]{1,0:T(8,128)(2,1)S(1)}, u32[]{:S(2)}, u32[]{:S(2)}) %collective-permute-start.6) | collective-permute-done | bytes 393248 | tf_op jit(solution)/shard_map/ppermute | solution.py:276
  17.5 3.0 %collective-permute-done.2.refs_0_ = bf16[32,6144]{1,0:T(8,128)(2,1)S(1)} collective-permute-done((bf16[32,6144]{1,0:T(8,128)(2,1)S(1)}, bf16[32,6144]{1,0:T(8,128)(2,1)S(1)}, u32[]{:S(2)}, u32[]{:S(2)}) %collective-permute-start.2) | collective-permute-done | bytes 393248 | tf_op jit(solution)/shard_map/ppermute | solution.py:18
  20.4 7.7 %collective-permute-done.3.refs_1_ = bf16[32,6144]{1,0:T(8,128)(2,1)S(1)} collective-permute-done((bf16[32,6144]{1,0:T(8,128)(2,1)S(1)}, bf16[32,6144]{1,0:T(8,128)(2,1)S(1)}, u32[]{:S(2)}, u32[]{:S(2)}) %collective-permute-start.3) | collective-permute-done | bytes 393248 | tf_op jit(solution)/shard_map/ppermute | solution.py:18
  28.8 2.1 %collective-permute-start.10 = (bf16[16,6144]{1,0:T(8,128)(2,1)S(1)}, bf16[16,6144]{1,0:T(8,128)(2,1)S(1)}, u32[]{:S(2)}, u32[]{:S(2)}) collective-permute-start(bf16[16,6144]{1,0:T(8,128)(2,1)S(1)} %get-tuple-element.41), channel_id=1, source_target_pairs={{0,3},{1,2},{2,1},{3,0},{4,7},{5,6},{6,5},{7,4},{8,11},{9,10},{10,... | collective-permute-start | bytes 589832 | tf_op jit(solution)/shard_map/ppermute | solution.py:276
  30.8 9.3 %collective-permute-done.7.refs_0_ = bf16[32,6144]{1,0:T(8,128)(2,1)S(1)} collective-permute-done((bf16[32,6144]{1,0:T(8,128)(2,1)S(1)}, bf16[32,6144]{1,0:T(8,128)(2,1)S(1)}, u32[]{:S(2)}, u32[]{:S(2)}) %collective-permute-start.7) | collective-permute-done | bytes 393248 | tf_op jit(solution)/shard_map/ppermute | solution.py:276
  42.7 2.1 %collective-permute-start.14 = (bf16[16,6144]{1,0:T(8,128)(2,1)S(1)}, bf16[16,6144]{1,0:T(8,128)(2,1)S(1)}, u32[]{:S(2)}, u32[]{:S(2)}) collective-permute-start(bf16[16,6144]{1,0:T(8,128)(2,1)S(1)} %get-tuple-element.48), channel_id=1, source_target_pairs={{0,3},{1,2},{2,1},{3,0},{4,7},{5,6},{6,5},{7,4},{8,11},{9,10},{10,... | collective-permute-start | bytes 589832 | tf_op jit(solution)/shard_map/ppermute | solution.py:276
  44.8 10.7 %expert_hidden.2.hidden = bf16[256,1024]{1,0:T(8,128)(2,1)S(1)} custom-call(bf16[32,6144]{1,0:T(8,128)(2,1)S(1)} %collective-permute-done.7.refs_0_, bf16[32,6144]{1,0:T(8,128)(2,1)S(1)} %collective-permute-done.6.refs_1_, bf16[32,6144]{1,0:T(8,128)(2,1)S(1)} %collective-permute-done.8.refs_2_, bf16[32,6144]{1,0:T(8,128)(2,1)S(1)} %get-tuple-element.42.refs_3_, ...), custom_call_target="tpu_custom_call" | custom-call | flops 6442450944 | bytes 28311552 | tf_op jit(solution)/shard_map/expert_hidden/pallas_call | solution.py:212
  56.5 5.9 %expert_down.2 = (bf16[32,6144]{1,0:T(8,128)(2,1)S(1)}, bf16[96,6144]{1,0:T(8,128)(2,1)S(1)}, bf16[32,6144]{1,0:T(8,128)(2,1)S(1)}, bf16[96,6144]{1,0:T(8,128)(2,1)S(1)}) custom-call(bf16[256,1024]{1,0:T(8,128)(2,1)S(1)} %expert_hidden.2.hidden, bf16[1024,6144]{1,0:T(8,128)(2,1)} %bitcast.9), custom_call_target="tpu_custom_call" | custom-call | flops 3221225472 | bytes 18874368 | tf_op jit(solution)/shard_map/expert_down/pallas_call | solution.py:237
  62.4 4.5 %collective-permute-done.15.refs_0_ = bf16[32,6144]{1,0:T(8,128)(2,1)S(1)} collective-permute-done((bf16[32,6144]{1,0:T(8,128)(2,1)S(1)}, bf16[32,6144]{1,0:T(8,128)(2,1)S(1)}, u32[]{:S(2)}, u32[]{:S(2)}) %collective-permute-start.15) | collective-permute-done | bytes 393248 | tf_op jit(solution)/shard_map/ppermute | solution.py:276
  70.6 2.4 %collective-permute-start.17 = (bf16[32,6144]{1,0:T(8,128)(2,1)S(1)}, bf16[32,6144]{1,0:T(8,128)(2,1)S(1)}, u32[]{:S(2)}, u32[]{:S(2)}) collective-permute-start(bf16[32,6144]{1,0:T(8,128)(2,1)S(1)} %get-tuple-element.72), channel_id=1, source_target_pairs={{0,8},{1,9},{2,10},{3,11},{4,12},{5,13},{6,14},{7,15},{8,16},{9,17... | collective-permute-start | bytes 1179656 | tf_op jit(solution)/shard_map/ppermute | solution.py:276
  73.6 6.3 %collective-permute-done.20 = bf16[32,6144]{1,0:T(8,128)(2,1)S(1)} collective-permute-done((bf16[32,6144]{1,0:T(8,128)(2,1)S(1)}, bf16[32,6144]{1,0:T(8,128)(2,1)S(1)}, u32[]{:S(2)}, u32[]{:S(2)}) %collective-permute-start.20) | collective-permute-done | bytes 393248 | tf_op jit(solution)/shard_map/ppermute | solution.py:276
  79.9 2.8 %collective-permute-done.17.refs_4_ = bf16[32,6144]{1,0:T(8,128)(2,1)S(1)} collective-permute-done((bf16[32,6144]{1,0:T(8,128)(2,1)S(1)}, bf16[32,6144]{1,0:T(8,128)(2,1)S(1)}, u32[]{:S(2)}, u32[]{:S(2)}) %collective-permute-start.17) | collective-permute-done | bytes 393248 | tf_op jit(solution)/shard_map/ppermute | solution.py:276
  84.1 3.2 %collective-permute-start.21 = (bf16[32,6144]{1,0:T(8,128)(2,1)S(1)}, bf16[32,6144]{1,0:T(8,128)(2,1)S(1)}, u32[]{:S(2)}, u32[]{:S(2)}) collective-permute-start(bf16[32,6144]{1,0:T(8,128)(2,1)S(1)} %add_convert_fusion.4), channel_id=1, source_target_pairs={{0,11},{1,10},{2,9},{3,8},{4,15},{5,14},{6,13},{7,12},{8,19},{9,18... | collective-permute-start | bytes 1179656 | tf_op jit(solution)/shard_map/ppermute | solution.py:276
  87.3 10.7 %expert_hidden.3.hidden = bf16[256,1024]{1,0:T(8,128)(2,1)S(1)} custom-call(bf16[32,6144]{1,0:T(8,128)(2,1)S(1)} %collective-permute-done.15.refs_0_, bf16[32,6144]{1,0:T(8,128)(2,1)S(1)} %constant_dynamic-update-slice_fusion.2.refs_1_, bf16[32,6144]{1,0:T(8,128)(2,1)S(1)} %collective-permute-done.13.refs_2_, ...), custom_call_target="tpu_custom_call" | custom-call | flops 6442450944 | bytes 28311552 | tf_op jit(solution)/shard_map/expert_hidden/pallas_call | solution.py:212
  98.0 5.9 %expert_down.3 = (bf16[32,6144]{1,0:T(8,128)(2,1)S(1)}, bf16[96,6144]{1,0:T(8,128)(2,1)S(1)}, bf16[32,6144]{1,0:T(8,128)(2,1)S(1)}, bf16[96,6144]{1,0:T(8,128)(2,1)S(1)}) custom-call(bf16[256,1024]{1,0:T(8,128)(2,1)S(1)} %expert_hidden.3.hidden, bf16[1024,6144]{1,0:T(8,128)(2,1)} %bitcast.10), custom_call_target="tpu_custom_call" | custom-call | flops 3221225472 | bytes 18874368 | tf_op jit(solution)/shard_map/expert_down/pallas_call | solution.py:237
  107.6 3.3 %collective-permute-start.30 = (bf16[32,6144]{1,0:T(8,128)(2,1)S(1)}, bf16[32,6144]{1,0:T(8,128)(2,1)S(1)}, u32[]{:S(2)}, u32[]{:S(2)}) collective-permute-start(bf16[32,6144]{1,0:T(8,128)(2,1)S(1)} %add_convert_fusion.3), channel_id=1, source_target_pairs={{0,1},{1,0},{2,3},{3,2},{4,5},{5,4},{6,7},{7,6},{8,9},{9,8},{10,11... | collective-permute-start | bytes 1179656 | tf_op jit(solution)/shard_map/ppermute | solution.py:276
  112.2 3.2 %collective-permute-start.28 = (bf16[32,6144]{1,0:T(8,128)(2,1)S(1)}, bf16[32,6144]{1,0:T(8,128)(2,1)S(1)}, u32[]{:S(2)}, u32[]{:S(2)}) collective-permute-start(bf16[32,6144]{1,0:T(8,128)(2,1)S(1)} %get-tuple-element.69), channel_id=1, source_target_pairs={{0,9},{1,8},{2,11},{3,10},{4,13},{5,12},{6,15},{7,14},{8,17},{9,16... | collective-permute-start | bytes 1179656 | tf_op jit(solution)/shard_map/ppermute | solution.py:276
  115.4 5.4 %collective-permute-done.30 = bf16[32,6144]{1,0:T(8,128)(2,1)S(1)} collective-permute-done((bf16[32,6144]{1,0:T(8,128)(2,1)S(1)}, bf16[32,6144]{1,0:T(8,128)(2,1)S(1)}, u32[]{:S(2)}, u32[]{:S(2)}) %collective-permute-start.30) | collective-permute-done | bytes 393248 | tf_op jit(solution)/shard_map/ppermute | solution.py:276
  120.9 2.1 %collective-permute-start.31 = (bf16[32,6144]{1,0:T(8,128)(2,1)S(1)}, bf16[32,6144]{1,0:T(8,128)(2,1)S(1)}, u32[]{:S(2)}, u32[]{:S(2)}) collective-permute-start(bf16[32,6144]{1,0:T(8,128)(2,1)S(1)} %add_convert_fusion.2), channel_id=1, source_target_pairs={{0,11},{1,10},{2,9},{3,8},{4,15},{5,14},{6,13},{7,12},{8,19},{9,18... | collective-permute-start | bytes 1179656 | tf_op jit(solution)/shard_map/ppermute | solution.py:276
  123.0 8.5 %collective-permute-done.27.refs_7_ = bf16[32,6144]{1,0:T(8,128)(2,1)S(1)} collective-permute-done((bf16[32,6144]{1,0:T(8,128)(2,1)S(1)}, bf16[32,6144]{1,0:T(8,128)(2,1)S(1)}, u32[]{:S(2)}, u32[]{:S(2)}) %collective-permute-start.27) | collective-permute-done | bytes 393248 | tf_op jit(solution)/shard_map/ppermute | solution.py:276
  133.2 9.9 %collective-permute-done.31.refs_9_ = bf16[32,6144]{1,0:T(8,128)(2,1)S(1)} collective-permute-done((bf16[32,6144]{1,0:T(8,128)(2,1)S(1)}, bf16[32,6144]{1,0:T(8,128)(2,1)S(1)}, u32[]{:S(2)}, u32[]{:S(2)}) %collective-permute-start.31) | collective-permute-done | bytes 393248 | tf_op jit(solution)/shard_map/ppermute | solution.py:276
  143.0 2.0 %combine_rows.1 = bf16[128,6144]{1,0:T(8,128)(2,1)} custom-call(f32[2,128]{1,0:T(2,128)S(1)} %collective-permute-done.meta_ref, bf16[32,6144]{1,0:T(8,128)(2,1)S(1)} %collective-permute-done.2.refs_0_, bf16[32,6144]{1,0:T(8,128)(2,1)S(1)} %collective-permute-done.3.refs_1_, bf16[32,6144]{1,0:T(8,128)(2,1)S(1)} %collective-permute-done.4.refs_2_, ...), custom_call_target="tpu_custom_call" | custom-call | flops 100663296 | bytes 3932160 | tf_op jit(solution)/shard_map/combine_rows/pallas_call | solution.py:134
  (61 shorter events, 21.7 us)
Async XLA Ops:
  2.7 14.7 %collective-permute-start.6 = (bf16[32,6144]{1,0:T(8,128)(2,1)S(1)}, bf16[32,6144]{1,0:T(8,128)(2,1)S(1)}, u32[]{:S(2)}, u32[]{:S(2)}) collective-permute-start(bf16[32,6144]{1,0:T(8,128)(2,1)S(1)} %get-tuple-element.42.refs_3_), channel_id=1, source_target_pairs={{0,3},{1,2},{2,1},{3,0},{4,7},{5,6},{6,5},{7,4},{8,11},{9,10},{10,... | collective-permute-start | bytes 1179656 | tf_op jit(solution)/shard_map/ppermute | solution.py:276
  7.5 12.9 %collective-permute-start.2 = (bf16[32,6144]{1,0:T(8,128)(2,1)S(1)}, bf16[32,6144]{1,0:T(8,128)(2,1)S(1)}, u32[]{:S(2)}, u32[]{:S(2)}) collective-permute-start(bf16[32,6144]{1,0:T(8,128)(2,1)S(1)} %get-tuple-element.68), channel_id=1, source_target_pairs={{0,8},{8,16},{16,24},{24,0},{1,9},{9,17},{17,25},{25,1},{2,10},{10... | collective-permute-start | bytes 1179656 | tf_op jit(solution)/shard_map/ppermute | solution.py:18
  9.1 19.0 %collective-permute-start.3 = (bf16[32,6144]{1,0:T(8,128)(2,1)S(1)}, bf16[32,6144]{1,0:T(8,128)(2,1)S(1)}, u32[]{:S(2)}, u32[]{:S(2)}) collective-permute-start(bf16[32,6144]{1,0:T(8,128)(2,1)S(1)} %get-tuple-element.67), channel_id=1, source_target_pairs={{0,8},{8,16},{16,24},{24,0},{1,9},{9,17},{17,25},{25,1},{2,10},{10... | collective-permute-start | bytes 1179656 | tf_op jit(solution)/shard_map/ppermute | solution.py:18
  10.6 29.6 %collective-permute-start = (f32[2,128]{1,0:T(2,128)S(1)}, f32[2,128]{1,0:T(2,128)S(1)}, u32[]{:S(2)}, u32[]{:S(2)}) collective-permute-start(f32[2,128]{1,0:T(2,128)S(1)} %get-tuple-element.35), channel_id=1, source_target_pairs={{0,8},{8,16},{16,24},{24,0},{1,9},{9,17},{17,25},{25,1},{2,10},{10... | collective-permute-start | bytes 3080 | tf_op jit(solution)/shard_map/ppermute | solution.py:18
  12.1 18.8 %collective-permute-start.8 = (bf16[32,6144]{1,0:T(8,128)(2,1)S(1)}, bf16[32,6144]{1,0:T(8,128)(2,1)S(1)}, u32[]{:S(2)}, u32[]{:S(2)}) collective-permute-start(bf16[32,6144]{1,0:T(8,128)(2,1)S(1)} %get-tuple-element.42.refs_3_), channel_id=1, source_target_pairs={{0,1},{1,0},{2,3},{3,2},{4,5},{5,4},{6,7},{7,6},{8,9},{9,8},{10,11... | collective-permute-start | bytes 1179656 | tf_op jit(solution)/shard_map/ppermute | solution.py:276
  17.5 11.3 %collective-permute-start.9 = (bf16[32,6144]{1,0:T(8,128)(2,1)S(1)}, bf16[32,6144]{1,0:T(8,128)(2,1)S(1)}, u32[]{:S(2)}, u32[]{:S(2)}) collective-permute-start(bf16[32,6144]{1,0:T(8,128)(2,1)S(1)} %collective-permute-done.6.refs_1_), channel_id=1, source_target_pairs={{0,4},{4,0},{1,5},{5,1},{2,6},{6,2},{3,7},{7,3},{8,12},{12,8},{9,1... | collective-permute-start | bytes 1179656 | tf_op jit(solution)/shard_map/ppermute | solution.py:23
  28.1 12.1 %collective-permute-start.7 = (bf16[32,6144]{1,0:T(8,128)(2,1)S(1)}, bf16[32,6144]{1,0:T(8,128)(2,1)S(1)}, u32[]{:S(2)}, u32[]{:S(2)}) collective-permute-start(bf16[32,6144]{1,0:T(8,128)(2,1)S(1)} %collective-permute-done.6.refs_1_), channel_id=1, source_target_pairs={{0,1},{1,0},{2,3},{3,2},{4,5},{5,4},{6,7},{7,6},{8,9},{9,8},{10,11... | collective-permute-start | bytes 1179656 | tf_op jit(solution)/shard_map/ppermute | solution.py:276
  28.1 12.7 %collective-permute-start.4 = (bf16[32,6144]{1,0:T(8,128)(2,1)S(1)}, bf16[32,6144]{1,0:T(8,128)(2,1)S(1)}, u32[]{:S(2)}, u32[]{:S(2)}) collective-permute-start(bf16[32,6144]{1,0:T(8,128)(2,1)S(1)} %get-tuple-element.66), channel_id=1, source_target_pairs={{0,8},{8,16},{16,24},{24,0},{1,9},{9,17},{17,25},{25,1},{2,10},{10... | collective-permute-start | bytes 1179656 | tf_op jit(solution)/shard_map/ppermute | solution.py:18
  28.8 13.9 %collective-permute-start.10 = (bf16[16,6144]{1,0:T(8,128)(2,1)S(1)}, bf16[16,6144]{1,0:T(8,128)(2,1)S(1)}, u32[]{:S(2)}, u32[]{:S(2)}) collective-permute-start(bf16[16,6144]{1,0:T(8,128)(2,1)S(1)} %get-tuple-element.41), channel_id=1, source_target_pairs={{0,3},{1,2},{2,1},{3,0},{4,7},{5,6},{6,5},{7,4},{8,11},{9,10},{10,... | collective-permute-start | bytes 589832 | tf_op jit(solution)/shard_map/ppermute | solution.py:276
  30.8 13.9 %collective-permute-start.12 = (bf16[32,6144]{1,0:T(8,128)(2,1)S(1)}, bf16[32,6144]{1,0:T(8,128)(2,1)S(1)}, u32[]{:S(2)}, u32[]{:S(2)}) collective-permute-start(bf16[32,6144]{1,0:T(8,128)(2,1)S(1)} %collective-permute-done.8.refs_2_), channel_id=1, source_target_pairs={{0,4},{4,0},{1,5},{5,1},{2,6},{6,2},{3,7},{7,3},{8,12},{12,8},{9,1... | collective-permute-start | bytes 1179656 | tf_op jit(solution)/shard_map/ppermute | solution.py:23
  40.2 16.2 %collective-permute-start.5 = (bf16[32,6144]{1,0:T(8,128)(2,1)S(1)}, bf16[32,6144]{1,0:T(8,128)(2,1)S(1)}, u32[]{:S(2)}, u32[]{:S(2)}) collective-permute-start(bf16[32,6144]{1,0:T(8,128)(2,1)S(1)} %get-tuple-element.65), channel_id=1, source_target_pairs={{0,8},{8,16},{16,24},{24,0},{1,9},{9,17},{17,25},{25,1},{2,10},{10... | collective-permute-start | bytes 1179656 | tf_op jit(solution)/shard_map/ppermute | solution.py:18
  40.9 15.6 %collective-permute-start.13 = (bf16[32,6144]{1,0:T(8,128)(2,1)S(1)}, bf16[32,6144]{1,0:T(8,128)(2,1)S(1)}, u32[]{:S(2)}, u32[]{:S(2)}) collective-permute-start(bf16[32,6144]{1,0:T(8,128)(2,1)S(1)} %constant_dynamic-update-slice_fusion.refs_3_), channel_id=1, source_target_pairs={{0,1},{1,0},{2,3},{3,2},{4,5},{5,4},{6,7},{7,6},{8,9},{9,8},{10,11... | collective-permute-start | bytes 1179656 | tf_op jit(solution)/shard_map/ppermute | solution.py:276
  42.7 13.7 %collective-permute-start.14 = (bf16[16,6144]{1,0:T(8,128)(2,1)S(1)}, bf16[16,6144]{1,0:T(8,128)(2,1)S(1)}, u32[]{:S(2)}, u32[]{:S(2)}) collective-permute-start(bf16[16,6144]{1,0:T(8,128)(2,1)S(1)} %get-tuple-element.48), channel_id=1, source_target_pairs={{0,3},{1,2},{2,1},{3,0},{4,7},{5,6},{6,5},{7,4},{8,11},{9,10},{10,... | collective-permute-start | bytes 589832 | tf_op jit(solution)/shard_map/ppermute | solution.py:276
  68.7 11.2 %collective-permute-start.20 = (bf16[32,6144]{1,0:T(8,128)(2,1)S(1)}, bf16[32,6144]{1,0:T(8,128)(2,1)S(1)}, u32[]{:S(2)}, u32[]{:S(2)}) collective-permute-start(bf16[32,6144]{1,0:T(8,128)(2,1)S(1)} %add_convert_fusion.5), channel_id=1, source_target_pairs={{0,1},{1,0},{2,3},{3,2},{4,5},{5,4},{6,7},{7,6},{8,9},{9,8},{10,11... | collective-permute-start | bytes 1179656 | tf_op jit(solution)/shard_map/ppermute | solution.py:276
  70.6 12.1 %collective-permute-start.17 = (bf16[32,6144]{1,0:T(8,128)(2,1)S(1)}, bf16[32,6144]{1,0:T(8,128)(2,1)S(1)}, u32[]{:S(2)}, u32[]{:S(2)}) collective-permute-start(bf16[32,6144]{1,0:T(8,128)(2,1)S(1)} %get-tuple-element.72), channel_id=1, source_target_pairs={{0,8},{1,9},{2,10},{3,11},{4,12},{5,13},{6,14},{7,15},{8,16},{9,17... | collective-permute-start | bytes 1179656 | tf_op jit(solution)/shard_map/ppermute | solution.py:276
  73.1 11.0 %collective-permute-start.25 = (bf16[32,6144]{1,0:T(8,128)(2,1)S(1)}, bf16[32,6144]{1,0:T(8,128)(2,1)S(1)}, u32[]{:S(2)}, u32[]{:S(2)}) collective-permute-start(bf16[32,6144]{1,0:T(8,128)(2,1)S(1)} %constant_dynamic-update-slice_fusion.refs_3_), channel_id=1, source_target_pairs={{0,4},{4,0},{1,5},{5,1},{2,6},{6,2},{3,7},{7,3},{8,12},{12,8},{9,1... | collective-permute-start | bytes 1179656 | tf_op jit(solution)/shard_map/ppermute | solution.py:23
  73.1 14.2 %collective-permute-start.24 = (bf16[32,6144]{1,0:T(8,128)(2,1)S(1)}, bf16[32,6144]{1,0:T(8,128)(2,1)S(1)}, u32[]{:S(2)}, u32[]{:S(2)}) collective-permute-start(bf16[32,6144]{1,0:T(8,128)(2,1)S(1)} %collective-permute-done.13.refs_2_), channel_id=1, source_target_pairs={{0,4},{4,0},{1,5},{5,1},{2,6},{6,2},{3,7},{7,3},{8,12},{12,8},{9,1... | collective-permute-start | bytes 1179656 | tf_op jit(solution)/shard_map/ppermute | solution.py:23
  73.6 13.7 %collective-permute-start.23 = (bf16[32,6144]{1,0:T(8,128)(2,1)S(1)}, bf16[32,6144]{1,0:T(8,128)(2,1)S(1)}, u32[]{:S(2)}, u32[]{:S(2)}) collective-permute-start(bf16[32,6144]{1,0:T(8,128)(2,1)S(1)} %constant_dynamic-update-slice_fusion.2.refs_1_), channel_id=1, source_target_pairs={{0,4},{4,0},{1,5},{5,1},{2,6},{6,2},{3,7},{7,3},{8,12},{12,8},{9,1... | collective-permute-start | bytes 1179656 | tf_op jit(solution)/shard_map/ppermute | solution.py:23
  82.7 21.2 %collective-permute-start.18 = (bf16[32,6144]{1,0:T(8,128)(2,1)S(1)}, bf16[32,6144]{1,0:T(8,128)(2,1)S(1)}, u32[]{:S(2)}, u32[]{:S(2)}) collective-permute-start(bf16[32,6144]{1,0:T(8,128)(2,1)S(1)} %get-tuple-element.71), channel_id=1, source_target_pairs={{0,9},{1,8},{2,11},{3,10},{4,13},{5,12},{6,15},{7,14},{8,17},{9,16... | collective-permute-start | bytes 1179656 | tf_op jit(solution)/shard_map/ppermute | solution.py:276
  84.1 21.7 %collective-permute-start.21 = (bf16[32,6144]{1,0:T(8,128)(2,1)S(1)}, bf16[32,6144]{1,0:T(8,128)(2,1)S(1)}, u32[]{:S(2)}, u32[]{:S(2)}) collective-permute-start(bf16[32,6144]{1,0:T(8,128)(2,1)S(1)} %add_convert_fusion.4), channel_id=1, source_target_pairs={{0,11},{1,10},{2,9},{3,8},{4,15},{5,14},{6,13},{7,12},{8,19},{9,18... | collective-permute-start | bytes 1179656 | tf_op jit(solution)/shard_map/ppermute | solution.py:276
  107.6 13.2 %collective-permute-start.30 = (bf16[32,6144]{1,0:T(8,128)(2,1)S(1)}, bf16[32,6144]{1,0:T(8,128)(2,1)S(1)}, u32[]{:S(2)}, u32[]{:S(2)}) collective-permute-start(bf16[32,6144]{1,0:T(8,128)(2,1)S(1)} %add_convert_fusion.3), channel_id=1, source_target_pairs={{0,1},{1,0},{2,3},{3,2},{4,5},{5,4},{6,7},{7,6},{8,9},{9,8},{10,11... | collective-permute-start | bytes 1179656 | tf_op jit(solution)/shard_map/ppermute | solution.py:276
  111.3 20.3 %collective-permute-start.27 = (bf16[32,6144]{1,0:T(8,128)(2,1)S(1)}, bf16[32,6144]{1,0:T(8,128)(2,1)S(1)}, u32[]{:S(2)}, u32[]{:S(2)}) collective-permute-start(bf16[32,6144]{1,0:T(8,128)(2,1)S(1)} %get-tuple-element.70), channel_id=1, source_target_pairs={{0,8},{1,9},{2,10},{3,11},{4,12},{5,13},{6,14},{7,15},{8,16},{9,17... | collective-permute-start | bytes 1179656 | tf_op jit(solution)/shard_map/ppermute | solution.py:276
  112.2 21.0 %collective-permute-start.28 = (bf16[32,6144]{1,0:T(8,128)(2,1)S(1)}, bf16[32,6144]{1,0:T(8,128)(2,1)S(1)}, u32[]{:S(2)}, u32[]{:S(2)}) collective-permute-start(bf16[32,6144]{1,0:T(8,128)(2,1)S(1)} %get-tuple-element.69), channel_id=1, source_target_pairs={{0,9},{1,8},{2,11},{3,10},{4,13},{5,12},{6,15},{7,14},{8,17},{9,16... | collective-permute-start | bytes 1179656 | tf_op jit(solution)/shard_map/ppermute | solution.py:276
  120.9 22.1 %collective-permute-start.31 = (bf16[32,6144]{1,0:T(8,128)(2,1)S(1)}, bf16[32,6144]{1,0:T(8,128)(2,1)S(1)}, u32[]{:S(2)}, u32[]{:S(2)}) collective-permute-start(bf16[32,6144]{1,0:T(8,128)(2,1)S(1)} %add_convert_fusion.2), channel_id=1, source_target_pairs={{0,11},{1,10},{2,9},{3,8},{4,15},{5,14},{6,13},{7,12},{8,19},{9,18... | collective-permute-start | bytes 1179656 | tf_op jit(solution)/shard_map/ppermute | solution.py:276
  (9 other events, 47.1 us)

commit v2 on v1

--- a/solution.py
+++ b/solution.py
@@ -10,7 +10,7 @@
 MIB = 2**20
 VMEM_HIDDEN = 34
 VMEM_DOWN = 24
-PIECES = 4
+PIECES, PIECES_OF = (2, 1, 2, 3), 8
 
 
 def next_section(block):
@@ -110,7 +110,6 @@
     inputs, refs = refs[:pieces], refs[pieces:]
     arrived, (out, sums) = refs[:-2], refs[-2:]
     rows, width = out.shape
-    each = rows // pieces
     first = 0
     for k, size in enumerate(sizes):
         total = sum(part[...].astype(jnp.float32) for part in arrived[3 * k : 3 * k + 3])
@@ -121,10 +120,12 @@
     spread = jnp.where(slot == place, 1.0, 0.0).astype(jnp.bfloat16)
     for start in range(0, width, step):
         branch = own * jnp.dot(spread, sums[:, start : start + step], preferred_element_type=jnp.float32)
-        for p, piece in enumerate(inputs):
-            mine = slice(p * each, (p + 1) * each)
+        done = 0
+        for piece in inputs:
+            mine = slice(done, done + piece.shape[0])
             x = piece[:, start : start + step].astype(jnp.float32)
             out[mine, start : start + step] = (x + branch[mine]).astype(jnp.bfloat16)
+            done += piece.shape[0]
 
 
 def combine(inputs, meta, arrived):
@@ -207,7 +208,7 @@
 def expert_hidden(blocks, gate_m, up_m):
     rows, width = blocks[0].shape
     hidden = gate_m.shape[1]
-    cols, parts = 256, 4
+    cols, parts = 256, 1
     vmem, stays = pl.BlockSpec(memory_space=pltpu.VMEM), pl.BlockSpec(memory_space=pltpu.HBM)
     return pl.pallas_call(
         functools.partial(hidden_kernel, cols, parts),
@@ -286,13 +287,18 @@
 
 def per_device(hidden_in, norm_gain, w_gate, w_up, w_down, expert_ids, gate_weights):
     rows = hidden_in.shape[0]
-    size, each = rows // 4, rows // PIECES
+    size = rows // 4
     meta, *packed = pack(hidden_in, norm_gain, expert_ids.T, gate_weights.T, [size, size // 2, size // 2])
     meta_before = next_section(meta)
     halves = [packed[0], jnp.concatenate(packed[1:], axis=0)]
     swapped = other_core(packed[0])
     early = after(hidden_in, swapped)
-    inputs = [next_section(early[p * each : (p + 1) * each]) for p in range(PIECES)]
+
+    def hand_on(block, p):
+        first = rows * sum(PIECES[:p]) // PIECES_OF
+        return next_section(block[first : first + rows * PIECES[p] // PIECES_OF])
+
+    inputs = [hand_on(early, p) for p in range(len(PIECES))]
 
     def expert_hidden_of(blocks, theirs):
         return expert_hidden(blocks + theirs, w_gate[0], w_up[0])
@@ -311,13 +317,14 @@
     far = route(after(cross, *inputs[:2]), chip(1))
     cross_swapped = other_core(cross)
     cross_next = [route(after(block, cross_swapped), chip(3)) for block in packed[1:]]
-    near_next = route(after(halves[1], cross_swapped), chip(1))
+    near_next = route(after(halves[1], cross_swapped, cross_next[0]), chip(1))
     mine = [far, cross, near, after(packed[0], inputs[2], cross_next[0], meta_before)]
     hidden = expert_hidden_of(mine, [other_core(far), cross_swapped, other_core(near), swapped])
     cross_next = jnp.concatenate([after(block, hidden) for block in cross_next], axis=0)
     far_next = route(after(cross_next, hidden), chip(1))
-    terms = expert_down(after(hidden, near_next, inputs[3]), w_down[0])
-    arrived = scatter([after(term, far_next) for term in terms], True)
+    keep_first, keep_rest, send_first, send_rest = expert_down(after(hidden, near_next, inputs[3]), w_down[0])
+    send_first, send_rest = after(send_first, far_next), after(send_rest, far_next)
+    arrived = scatter([keep_first, keep_rest, send_first, send_rest], True)
 
     mine = [far_next, cross_next, near_next, halves[1]]
     hidden = expert_hidden_of(mine, [other_core(block) for block in mine])

time: 146 us -> 143 us (0.979)
  waiting for transfers between devices: 72.3 us -> 64.6 us
  starting transfers between devices: 33.9 us -> 39.2 us
    ppermute x5, waiting for transfers between devices: 10.7 us -> 7.18 us  [next_section(): lax.ppermute(block, 'pipe', [(i, (i + 1) % count) for i in range(count)])]
    ppermute x15, starting transfers between devices: 26 us -> 29.4 us  [route(): return lax.ppermute(block, ('pipe', 'expert', 'dp'), pairs)]
    ppermute x15, waiting for transfers between devices: 57.9 us -> 55 us  [route(): return lax.ppermute(block, ('pipe', 'expert', 'dp'), pairs)]
    ppermute x5, starting transfers between devices: 5.83 us -> 7.67 us  [next_section(): lax.ppermute(block, 'pipe', [(i, (i + 1) % count) for i in range(count)])]
  transfers between devices with their start and end apart: 32 -> 32, of which waited for: 17 -> 16; matrix products, arithmetic and copies ran while one was open for 1% -> 1% of each run, Pallas kernels for 23% -> 23%
where the time goes in v2:
time: 143 us; the launch traced here: 142 us
  waiting for transfers between devices  64.6 us (45%)
  starting transfers between devices  39.2 us (27%)
  Pallas kernels  36.5 us (26%)
    ppermute x15, waiting for transfers between devices, route(): return lax.ppermute(block, ('pipe', 'expert', 'dp'), pairs)  55 us
    ppermute x15, starting transfers between devices, route(): return lax.ppermute(block, ('pipe', 'expert', 'dp'), pairs)  29.4 us
    pallas_call x2, Pallas kernels, expert_hidden(): pl.pallas_call(functools.partial(hidden_kernel, cols, parts), out_shape=j...  20.5 us
    pallas_call x2, Pallas kernels, expert_down(): pl.pallas_call(functools.partial(down_kernel, cols), out_shape=[first, re...  11.8 us
    ppermute x5, starting transfers between devices, next_section(): lax.ppermute(block, 'pipe', [(i, (i + 1) % count) for i in range(count)])  7.67 us
    ppermute x5, waiting for transfers between devices, next_section(): lax.ppermute(block, 'pipe', [(i, (i + 1) % count) for i in range(count)])  7.18 us
  transfers between devices with their start and end apart: 32, of which 16 were waited for; matrix products, arithmetic and copies ran while one was open for 1% of the time, Pallas kernels for 23%

profile of v2, /device:TPU:0, one launch (start us, length us, event | category | flops | bytes accessed | tf_op | source)
XLA Modules:
  0.0 141.7 jit_solution(11722007804261188010)
XLA Ops:
  0.0 2.2 %pack_rows.1 = (f32[2,128]{1,0:T(2,128)S(1)}, bf16[32,6144]{1,0:T(8,128)(2,1)S(1)}, bf16[16,6144]{1,0:T(8,128)(2,1)S(1)}, bf16[16,6144]{1,0:T(8,128)(2,1)S(1)}) custom-call(bf16[128,6144]{1,0:T(8,128)(2,1)} %x_hbm.1, f32[1,6144]{1,0:T(1,128)} %gain_hbm.1, s32[2,128]{1,0:T(2,128)} %bitcast.11, f32[2,128]{1,0:T(2,128)} %bitcast.12), custom_call_target="tpu_custom_call" | custom-call | flops 100663296 | bytes 2359296 | tf_op jit(solution)/shard_map/pack_rows/pallas_call | solution.py:89
  2.7 4.7 %collective-permute-start.6 = (bf16[32,6144]{1,0:T(8,128)(2,1)S(1)}, bf16[32,6144]{1,0:T(8,128)(2,1)S(1)}, u32[]{:S(2)}, u32[]{:S(2)}) collective-permute-start(bf16[32,6144]{1,0:T(8,128)(2,1)S(1)} %get-tuple-element.40.refs_3_), channel_id=1, source_target_pairs={{0,3},{1,2},{2,1},{3,0},{4,7},{5,6},{6,5},{7,4},{8,11},{9,10},{10,... | collective-permute-start | bytes 1179656 | tf_op jit(solution)/shard_map/ppermute | solution.py:277
  12.1 5.4 %collective-permute-done.6.refs_1_ = bf16[32,6144]{1,0:T(8,128)(2,1)S(1)} collective-permute-done((bf16[32,6144]{1,0:T(8,128)(2,1)S(1)}, bf16[32,6144]{1,0:T(8,128)(2,1)S(1)}, u32[]{:S(2)}, u32[]{:S(2)}) %collective-permute-start.6) | collective-permute-done | bytes 393248 | tf_op jit(solution)/shard_map/ppermute | solution.py:277
  17.5 6.4 %collective-permute-done.3.refs_1_ = bf16[16,6144]{1,0:T(8,128)(2,1)S(1)} collective-permute-done((bf16[16,6144]{1,0:T(8,128)(2,1)S(1)}, bf16[16,6144]{1,0:T(8,128)(2,1)S(1)}, u32[]{:S(2)}, u32[]{:S(2)}) %collective-permute-start.3) | collective-permute-done | bytes 196640 | tf_op jit(solution)/shard_map/ppermute | solution.py:18
  26.9 2.5 %collective-permute-start.10 = (bf16[16,6144]{1,0:T(8,128)(2,1)S(1)}, bf16[16,6144]{1,0:T(8,128)(2,1)S(1)}, u32[]{:S(2)}, u32[]{:S(2)}) collective-permute-start(bf16[16,6144]{1,0:T(8,128)(2,1)S(1)} %get-tuple-element.39), channel_id=1, source_target_pairs={{0,3},{1,2},{2,1},{3,0},{4,7},{5,6},{6,5},{7,4},{8,11},{9,10},{10,... | collective-permute-start | bytes 589832 | tf_op jit(solution)/shard_map/ppermute | solution.py:277
  29.4 5.7 %collective-permute-done.7.refs_0_ = bf16[32,6144]{1,0:T(8,128)(2,1)S(1)} collective-permute-done((bf16[32,6144]{1,0:T(8,128)(2,1)S(1)}, bf16[32,6144]{1,0:T(8,128)(2,1)S(1)}, u32[]{:S(2)}, u32[]{:S(2)}) %collective-permute-start.7) | collective-permute-done | bytes 393248 | tf_op jit(solution)/shard_map/ppermute | solution.py:277
  37.5 2.5 %collective-permute-start.14 = (bf16[16,6144]{1,0:T(8,128)(2,1)S(1)}, bf16[16,6144]{1,0:T(8,128)(2,1)S(1)}, u32[]{:S(2)}, u32[]{:S(2)}) collective-permute-start(bf16[16,6144]{1,0:T(8,128)(2,1)S(1)} %get-tuple-element.47), channel_id=1, source_target_pairs={{0,3},{1,2},{2,1},{3,0},{4,7},{5,6},{6,5},{7,4},{8,11},{9,10},{10,... | collective-permute-start | bytes 589832 | tf_op jit(solution)/shard_map/ppermute | solution.py:277
  41.6 10.2 %expert_hidden.2.hidden = bf16[256,1024]{1,0:T(8,128)(2,1)S(1)} custom-call(bf16[32,6144]{1,0:T(8,128)(2,1)S(1)} %collective-permute-done.7.refs_0_, bf16[32,6144]{1,0:T(8,128)(2,1)S(1)} %collective-permute-done.6.refs_1_, bf16[32,6144]{1,0:T(8,128)(2,1)S(1)} %collective-permute-done.8.refs_2_, bf16[32,6144]{1,0:T(8,128)(2,1)S(1)} %get-tuple-element.40.refs_3_, ...), custom_call_target="tpu_custom_call" | custom-call | flops 6442450944 | bytes 28311552 | tf_op jit(solution)/shard_map/expert_hidden/pallas_call | solution.py:213
  51.9 2.1 %collective-permute-start.15 = (bf16[32,6144]{1,0:T(8,128)(2,1)S(1)}, bf16[32,6144]{1,0:T(8,128)(2,1)S(1)}, u32[]{:S(2)}, u32[]{:S(2)}) collective-permute-start(bf16[32,6144]{1,0:T(8,128)(2,1)S(1)} %constant_dynamic-update-slice_fusion.2.refs_1_), channel_id=1, source_target_pairs={{0,1},{1,0},{2,3},{3,2},{4,5},{5,4},{6,7},{7,6},{8,9},{9,8},{10,11... | collective-permute-start | bytes 1179656 | tf_op jit(solution)/shard_map/ppermute | solution.py:277
  54.3 5.9 %expert_down.2 = (bf16[32,6144]{1,0:T(8,128)(2,1)S(1)}, bf16[96,6144]{1,0:T(8,128)(2,1)S(1)}, bf16[32,6144]{1,0:T(8,128)(2,1)S(1)}, bf16[96,6144]{1,0:T(8,128)(2,1)S(1)}) custom-call(bf16[256,1024]{1,0:T(8,128)(2,1)S(1)} %expert_hidden.2.hidden, bf16[1024,6144]{1,0:T(8,128)(2,1)} %bitcast.9), custom_call_target="tpu_custom_call" | custom-call | flops 3221225472 | bytes 18874368 | tf_op jit(solution)/shard_map/expert_down/pallas_call | solution.py:238
  60.2 2.4 %collective-permute-done.15.refs_0_ = bf16[32,6144]{1,0:T(8,128)(2,1)S(1)} collective-permute-done((bf16[32,6144]{1,0:T(8,128)(2,1)S(1)}, bf16[32,6144]{1,0:T(8,128)(2,1)S(1)}, u32[]{:S(2)}, u32[]{:S(2)}) %collective-permute-start.15) | collective-permute-done | bytes 393248 | tf_op jit(solution)/shard_map/ppermute | solution.py:277
  64.5 1.7 %collective-permute-start.20 = (bf16[32,6144]{1,0:T(8,128)(2,1)S(1)}, bf16[32,6144]{1,0:T(8,128)(2,1)S(1)}, u32[]{:S(2)}, u32[]{:S(2)}) collective-permute-start(bf16[32,6144]{1,0:T(8,128)(2,1)S(1)} %add_convert_fusion.5), channel_id=1, source_target_pairs={{0,1},{1,0},{2,3},{3,2},{4,5},{5,4},{6,7},{7,6},{8,9},{9,8},{10,11... | collective-permute-start | bytes 1179656 | tf_op jit(solution)/shard_map/ppermute | solution.py:277
  68.6 7.1 %collective-permute-done.20 = bf16[32,6144]{1,0:T(8,128)(2,1)S(1)} collective-permute-done((bf16[32,6144]{1,0:T(8,128)(2,1)S(1)}, bf16[32,6144]{1,0:T(8,128)(2,1)S(1)}, u32[]{:S(2)}, u32[]{:S(2)}) %collective-permute-start.20) | collective-permute-done | bytes 393248 | tf_op jit(solution)/shard_map/ppermute | solution.py:277
  75.7 2.8 %collective-permute-done.17.refs_4_ = bf16[32,6144]{1,0:T(8,128)(2,1)S(1)} collective-permute-done((bf16[32,6144]{1,0:T(8,128)(2,1)S(1)}, bf16[32,6144]{1,0:T(8,128)(2,1)S(1)}, u32[]{:S(2)}, u32[]{:S(2)}) %collective-permute-start.17) | collective-permute-done | bytes 393248 | tf_op jit(solution)/shard_map/ppermute | solution.py:277
  80.3 3.4 %collective-permute-start.21 = (bf16[32,6144]{1,0:T(8,128)(2,1)S(1)}, bf16[32,6144]{1,0:T(8,128)(2,1)S(1)}, u32[]{:S(2)}, u32[]{:S(2)}) collective-permute-start(bf16[32,6144]{1,0:T(8,128)(2,1)S(1)} %add_convert_fusion.4), channel_id=1, source_target_pairs={{0,11},{1,10},{2,9},{3,8},{4,15},{5,14},{6,13},{7,12},{8,19},{9,18... | collective-permute-start | bytes 1179656 | tf_op jit(solution)/shard_map/ppermute | solution.py:277
  83.7 10.2 %expert_hidden.3.hidden = bf16[256,1024]{1,0:T(8,128)(2,1)S(1)} custom-call(bf16[32,6144]{1,0:T(8,128)(2,1)S(1)} %collective-permute-done.15.refs_0_, bf16[32,6144]{1,0:T(8,128)(2,1)S(1)} %constant_dynamic-update-slice_fusion.2.refs_1_, bf16[32,6144]{1,0:T(8,128)(2,1)S(1)} %collective-permute-done.13.refs_2_, ...), custom_call_target="tpu_custom_call" | custom-call | flops 6442450944 | bytes 28311552 | tf_op jit(solution)/shard_map/expert_hidden/pallas_call | solution.py:213
  93.9 5.9 %expert_down.3 = (bf16[32,6144]{1,0:T(8,128)(2,1)S(1)}, bf16[96,6144]{1,0:T(8,128)(2,1)S(1)}, bf16[32,6144]{1,0:T(8,128)(2,1)S(1)}, bf16[96,6144]{1,0:T(8,128)(2,1)S(1)}) custom-call(bf16[256,1024]{1,0:T(8,128)(2,1)S(1)} %expert_hidden.3.hidden, bf16[1024,6144]{1,0:T(8,128)(2,1)} %bitcast.10), custom_call_target="tpu_custom_call" | custom-call | flops 3221225472 | bytes 18874368 | tf_op jit(solution)/shard_map/expert_down/pallas_call | solution.py:238
  99.9 4.4 %collective-permute-done.21.refs_6_ = bf16[32,6144]{1,0:T(8,128)(2,1)S(1)} collective-permute-done((bf16[32,6144]{1,0:T(8,128)(2,1)S(1)}, bf16[32,6144]{1,0:T(8,128)(2,1)S(1)}, u32[]{:S(2)}, u32[]{:S(2)}) %collective-permute-start.21) | collective-permute-done | bytes 393248 | tf_op jit(solution)/shard_map/ppermute | solution.py:277
  108.1 4.6 %collective-permute-start.28 = (bf16[32,6144]{1,0:T(8,128)(2,1)S(1)}, bf16[32,6144]{1,0:T(8,128)(2,1)S(1)}, u32[]{:S(2)}, u32[]{:S(2)}) collective-permute-start(bf16[32,6144]{1,0:T(8,128)(2,1)S(1)} %get-tuple-element.63), channel_id=1, source_target_pairs={{0,9},{1,8},{2,11},{3,10},{4,13},{5,12},{6,15},{7,14},{8,17},{9,16... | collective-permute-start | bytes 1179656 | tf_op jit(solution)/shard_map/ppermute | solution.py:277
  112.7 5.4 %collective-permute-done.30 = bf16[32,6144]{1,0:T(8,128)(2,1)S(1)} collective-permute-done((bf16[32,6144]{1,0:T(8,128)(2,1)S(1)}, bf16[32,6144]{1,0:T(8,128)(2,1)S(1)}, u32[]{:S(2)}, u32[]{:S(2)}) %collective-permute-start.30) | collective-permute-done | bytes 393248 | tf_op jit(solution)/shard_map/ppermute | solution.py:277
  118.2 1.7 %collective-permute-start.31 = (bf16[32,6144]{1,0:T(8,128)(2,1)S(1)}, bf16[32,6144]{1,0:T(8,128)(2,1)S(1)}, u32[]{:S(2)}, u32[]{:S(2)}) collective-permute-start(bf16[32,6144]{1,0:T(8,128)(2,1)S(1)} %add_convert_fusion.2), channel_id=1, source_target_pairs={{0,11},{1,10},{2,9},{3,8},{4,15},{5,14},{6,13},{7,12},{8,19},{9,18... | collective-permute-start | bytes 1179656 | tf_op jit(solution)/shard_map/ppermute | solution.py:277
  119.9 8.7 %collective-permute-done.27.refs_7_ = bf16[32,6144]{1,0:T(8,128)(2,1)S(1)} collective-permute-done((bf16[32,6144]{1,0:T(8,128)(2,1)S(1)}, bf16[32,6144]{1,0:T(8,128)(2,1)S(1)}, u32[]{:S(2)}, u32[]{:S(2)}) %collective-permute-start.27) | collective-permute-done | bytes 393248 | tf_op jit(solution)/shard_map/ppermute | solution.py:277
  129.7 10.1 %collective-permute-done.31.refs_9_ = bf16[32,6144]{1,0:T(8,128)(2,1)S(1)} collective-permute-done((bf16[32,6144]{1,0:T(8,128)(2,1)S(1)}, bf16[32,6144]{1,0:T(8,128)(2,1)S(1)}, u32[]{:S(2)}, u32[]{:S(2)}) %collective-permute-start.31) | collective-permute-done | bytes 393248 | tf_op jit(solution)/shard_map/ppermute | solution.py:277
  139.7 2.0 %combine_rows.1 = bf16[128,6144]{1,0:T(8,128)(2,1)} custom-call(f32[2,128]{1,0:T(2,128)S(1)} %collective-permute-done.meta_ref, bf16[32,6144]{1,0:T(8,128)(2,1)S(1)} %collective-permute-done.2.refs_0_, bf16[16,6144]{1,0:T(8,128)(2,1)S(1)} %collective-permute-done.3.refs_1_, bf16[32,6144]{1,0:T(8,128)(2,1)S(1)} %collective-permute-done.4.refs_2_, ...), custom_call_target="tpu_custom_call" | custom-call | flops 100663296 | bytes 3932160 | tf_op jit(solution)/shard_map/combine_rows/pallas_call | solution.py:135
  (63 shorter events, 23.6 us)
Async XLA Ops:
  2.7 14.7 %collective-permute-start.6 = (bf16[32,6144]{1,0:T(8,128)(2,1)S(1)}, bf16[32,6144]{1,0:T(8,128)(2,1)S(1)}, u32[]{:S(2)}, u32[]{:S(2)}) collective-permute-start(bf16[32,6144]{1,0:T(8,128)(2,1)S(1)} %get-tuple-element.40.refs_3_), channel_id=1, source_target_pairs={{0,3},{1,2},{2,1},{3,0},{4,7},{5,6},{6,5},{7,4},{8,11},{9,10},{10,... | collective-permute-start | bytes 1179656 | tf_op jit(solution)/shard_map/ppermute | solution.py:277
  7.5 16.4 %collective-permute-start.2 = (bf16[32,6144]{1,0:T(8,128)(2,1)S(1)}, bf16[32,6144]{1,0:T(8,128)(2,1)S(1)}, u32[]{:S(2)}, u32[]{:S(2)}) collective-permute-start(bf16[32,6144]{1,0:T(8,128)(2,1)S(1)} %get-tuple-element.62), channel_id=1, source_target_pairs={{0,8},{8,16},{16,24},{24,0},{1,9},{9,17},{17,25},{25,1},{2,10},{10... | collective-permute-start | bytes 1179656 | tf_op jit(solution)/shard_map/ppermute | solution.py:18
  9.0 14.8 %collective-permute-start.3 = (bf16[16,6144]{1,0:T(8,128)(2,1)S(1)}, bf16[16,6144]{1,0:T(8,128)(2,1)S(1)}, u32[]{:S(2)}, u32[]{:S(2)}) collective-permute-start(bf16[16,6144]{1,0:T(8,128)(2,1)S(1)} %slice.31), channel_id=1, source_target_pairs={{0,8},{8,16},{16,24},{24,0},{1,9},{9,17},{17,25},{25,1},{2,10},{10... | collective-permute-start | bytes 589832 | tf_op jit(solution)/shard_map/ppermute | solution.py:18
  10.6 24.6 %collective-permute-start = (f32[2,128]{1,0:T(2,128)S(1)}, f32[2,128]{1,0:T(2,128)S(1)}, u32[]{:S(2)}, u32[]{:S(2)}) collective-permute-start(f32[2,128]{1,0:T(2,128)S(1)} %get-tuple-element.33), channel_id=1, source_target_pairs={{0,8},{8,16},{16,24},{24,0},{1,9},{9,17},{17,25},{25,1},{2,10},{10... | collective-permute-start | bytes 3080 | tf_op jit(solution)/shard_map/ppermute | solution.py:18
  12.1 17.3 %collective-permute-start.8 = (bf16[32,6144]{1,0:T(8,128)(2,1)S(1)}, bf16[32,6144]{1,0:T(8,128)(2,1)S(1)}, u32[]{:S(2)}, u32[]{:S(2)}) collective-permute-start(bf16[32,6144]{1,0:T(8,128)(2,1)S(1)} %get-tuple-element.40.refs_3_), channel_id=1, source_target_pairs={{0,1},{1,0},{2,3},{3,2},{4,5},{5,4},{6,7},{7,6},{8,9},{9,8},{10,11... | collective-permute-start | bytes 1179656 | tf_op jit(solution)/shard_map/ppermute | solution.py:277
  23.8 11.2 %collective-permute-start.7 = (bf16[32,6144]{1,0:T(8,128)(2,1)S(1)}, bf16[32,6144]{1,0:T(8,128)(2,1)S(1)}, u32[]{:S(2)}, u32[]{:S(2)}) collective-permute-start(bf16[32,6144]{1,0:T(8,128)(2,1)S(1)} %collective-permute-done.6.refs_1_), channel_id=1, source_target_pairs={{0,1},{1,0},{2,3},{3,2},{4,5},{5,4},{6,7},{7,6},{8,9},{9,8},{10,11... | collective-permute-start | bytes 1179656 | tf_op jit(solution)/shard_map/ppermute | solution.py:277
  25.4 12.1 %collective-permute-start.4 = (bf16[32,6144]{1,0:T(8,128)(2,1)S(1)}, bf16[32,6144]{1,0:T(8,128)(2,1)S(1)}, u32[]{:S(2)}, u32[]{:S(2)}) collective-permute-start(bf16[32,6144]{1,0:T(8,128)(2,1)S(1)} %get-tuple-element.61), channel_id=1, source_target_pairs={{0,8},{8,16},{16,24},{24,0},{1,9},{9,17},{17,25},{25,1},{2,10},{10... | collective-permute-start | bytes 1179656 | tf_op jit(solution)/shard_map/ppermute | solution.py:18
  26.9 14.7 %collective-permute-start.10 = (bf16[16,6144]{1,0:T(8,128)(2,1)S(1)}, bf16[16,6144]{1,0:T(8,128)(2,1)S(1)}, u32[]{:S(2)}, u32[]{:S(2)}) collective-permute-start(bf16[16,6144]{1,0:T(8,128)(2,1)S(1)} %get-tuple-element.39), channel_id=1, source_target_pairs={{0,3},{1,2},{2,1},{3,0},{4,7},{5,6},{6,5},{7,4},{8,11},{9,10},{10,... | collective-permute-start | bytes 589832 | tf_op jit(solution)/shard_map/ppermute | solution.py:277
  29.4 12.2 %collective-permute-start.12 = (bf16[32,6144]{1,0:T(8,128)(2,1)S(1)}, bf16[32,6144]{1,0:T(8,128)(2,1)S(1)}, u32[]{:S(2)}, u32[]{:S(2)}) collective-permute-start(bf16[32,6144]{1,0:T(8,128)(2,1)S(1)} %collective-permute-done.8.refs_2_), channel_id=1, source_target_pairs={{0,4},{4,0},{1,5},{5,1},{2,6},{6,2},{3,7},{7,3},{8,12},{12,8},{9,1... | collective-permute-start | bytes 1179656 | tf_op jit(solution)/shard_map/ppermute | solution.py:23
  35.1 18.8 %collective-permute-start.5 = (bf16[48,6144]{1,0:T(8,128)(2,1)S(1)}, bf16[48,6144]{1,0:T(8,128)(2,1)S(1)}, u32[]{:S(2)}, u32[]{:S(2)}) collective-permute-start(bf16[48,6144]{1,0:T(8,128)(2,1)S(1)} %slice.33), channel_id=1, source_target_pairs={{0,8},{8,16},{16,24},{24,0},{1,9},{9,17},{17,25},{25,1},{2,10},{10... | collective-permute-start | bytes 1769480 | tf_op jit(solution)/shard_map/ppermute | solution.py:18
  37.5 14.4 %collective-permute-start.14 = (bf16[16,6144]{1,0:T(8,128)(2,1)S(1)}, bf16[16,6144]{1,0:T(8,128)(2,1)S(1)}, u32[]{:S(2)}, u32[]{:S(2)}) collective-permute-start(bf16[16,6144]{1,0:T(8,128)(2,1)S(1)} %get-tuple-element.47), channel_id=1, source_target_pairs={{0,3},{1,2},{2,1},{3,0},{4,7},{5,6},{6,5},{7,4},{8,11},{9,10},{10,... | collective-permute-start | bytes 589832 | tf_op jit(solution)/shard_map/ppermute | solution.py:277
  41.6 12.7 %collective-permute-start.13 = (bf16[32,6144]{1,0:T(8,128)(2,1)S(1)}, bf16[32,6144]{1,0:T(8,128)(2,1)S(1)}, u32[]{:S(2)}, u32[]{:S(2)}) collective-permute-start(bf16[32,6144]{1,0:T(8,128)(2,1)S(1)} %constant_dynamic-update-slice_fusion.refs_3_), channel_id=1, source_target_pairs={{0,1},{1,0},{2,3},{3,2},{4,5},{5,4},{6,7},{7,6},{8,9},{9,8},{10,11... | collective-permute-start | bytes 1179656 | tf_op jit(solution)/shard_map/ppermute | solution.py:277
  51.9 10.7 %collective-permute-start.15 = (bf16[32,6144]{1,0:T(8,128)(2,1)S(1)}, bf16[32,6144]{1,0:T(8,128)(2,1)S(1)}, u32[]{:S(2)}, u32[]{:S(2)}) collective-permute-start(bf16[32,6144]{1,0:T(8,128)(2,1)S(1)} %constant_dynamic-update-slice_fusion.2.refs_1_), channel_id=1, source_target_pairs={{0,1},{1,0},{2,3},{3,2},{4,5},{5,4},{6,7},{7,6},{8,9},{9,8},{10,11... | collective-permute-start | bytes 1179656 | tf_op jit(solution)/shard_map/ppermute | solution.py:277
  64.5 11.2 %collective-permute-start.20 = (bf16[32,6144]{1,0:T(8,128)(2,1)S(1)}, bf16[32,6144]{1,0:T(8,128)(2,1)S(1)}, u32[]{:S(2)}, u32[]{:S(2)}) collective-permute-start(bf16[32,6144]{1,0:T(8,128)(2,1)S(1)} %add_convert_fusion.5), channel_id=1, source_target_pairs={{0,1},{1,0},{2,3},{3,2},{4,5},{5,4},{6,7},{7,6},{8,9},{9,8},{10,11... | collective-permute-start | bytes 1179656 | tf_op jit(solution)/shard_map/ppermute | solution.py:277
  66.5 12.0 %collective-permute-start.17 = (bf16[32,6144]{1,0:T(8,128)(2,1)S(1)}, bf16[32,6144]{1,0:T(8,128)(2,1)S(1)}, u32[]{:S(2)}, u32[]{:S(2)}) collective-permute-start(bf16[32,6144]{1,0:T(8,128)(2,1)S(1)} %get-tuple-element.66), channel_id=1, source_target_pairs={{0,8},{1,9},{2,10},{3,11},{4,12},{5,13},{6,14},{7,15},{8,16},{9,17... | collective-permute-start | bytes 1179656 | tf_op jit(solution)/shard_map/ppermute | solution.py:277
  68.0 12.2 %collective-permute-start.25 = (bf16[32,6144]{1,0:T(8,128)(2,1)S(1)}, bf16[32,6144]{1,0:T(8,128)(2,1)S(1)}, u32[]{:S(2)}, u32[]{:S(2)}) collective-permute-start(bf16[32,6144]{1,0:T(8,128)(2,1)S(1)} %constant_dynamic-update-slice_fusion.refs_3_), channel_id=1, source_target_pairs={{0,4},{4,0},{1,5},{5,1},{2,6},{6,2},{3,7},{7,3},{8,12},{12,8},{9,1... | collective-permute-start | bytes 1179656 | tf_op jit(solution)/shard_map/ppermute | solution.py:23
  68.1 15.6 %collective-permute-start.24 = (bf16[32,6144]{1,0:T(8,128)(2,1)S(1)}, bf16[32,6144]{1,0:T(8,128)(2,1)S(1)}, u32[]{:S(2)}, u32[]{:S(2)}) collective-permute-start(bf16[32,6144]{1,0:T(8,128)(2,1)S(1)} %collective-permute-done.13.refs_2_), channel_id=1, source_target_pairs={{0,4},{4,0},{1,5},{5,1},{2,6},{6,2},{3,7},{7,3},{8,12},{12,8},{9,1... | collective-permute-start | bytes 1179656 | tf_op jit(solution)/shard_map/ppermute | solution.py:23
  68.6 15.1 %collective-permute-start.23 = (bf16[32,6144]{1,0:T(8,128)(2,1)S(1)}, bf16[32,6144]{1,0:T(8,128)(2,1)S(1)}, u32[]{:S(2)}, u32[]{:S(2)}) collective-permute-start(bf16[32,6144]{1,0:T(8,128)(2,1)S(1)} %constant_dynamic-update-slice_fusion.2.refs_1_), channel_id=1, source_target_pairs={{0,4},{4,0},{1,5},{5,1},{2,6},{6,2},{3,7},{7,3},{8,12},{12,8},{9,1... | collective-permute-start | bytes 1179656 | tf_op jit(solution)/shard_map/ppermute | solution.py:23
  78.5 21.3 %collective-permute-start.18 = (bf16[32,6144]{1,0:T(8,128)(2,1)S(1)}, bf16[32,6144]{1,0:T(8,128)(2,1)S(1)}, u32[]{:S(2)}, u32[]{:S(2)}) collective-permute-start(bf16[32,6144]{1,0:T(8,128)(2,1)S(1)} %get-tuple-element.65), channel_id=1, source_target_pairs={{0,9},{1,8},{2,11},{3,10},{4,13},{5,12},{6,15},{7,14},{8,17},{9,16... | collective-permute-start | bytes 1179656 | tf_op jit(solution)/shard_map/ppermute | solution.py:277
  80.3 24.0 %collective-permute-start.21 = (bf16[32,6144]{1,0:T(8,128)(2,1)S(1)}, bf16[32,6144]{1,0:T(8,128)(2,1)S(1)}, u32[]{:S(2)}, u32[]{:S(2)}) collective-permute-start(bf16[32,6144]{1,0:T(8,128)(2,1)S(1)} %add_convert_fusion.4), channel_id=1, source_target_pairs={{0,11},{1,10},{2,9},{3,8},{4,15},{5,14},{6,13},{7,12},{8,19},{9,18... | collective-permute-start | bytes 1179656 | tf_op jit(solution)/shard_map/ppermute | solution.py:277
  106.1 12.0 %collective-permute-start.30 = (bf16[32,6144]{1,0:T(8,128)(2,1)S(1)}, bf16[32,6144]{1,0:T(8,128)(2,1)S(1)}, u32[]{:S(2)}, u32[]{:S(2)}) collective-permute-start(bf16[32,6144]{1,0:T(8,128)(2,1)S(1)} %add_convert_fusion.3), channel_id=1, source_target_pairs={{0,1},{1,0},{2,3},{3,2},{4,5},{5,4},{6,7},{7,6},{8,9},{9,8},{10,11... | collective-permute-start | bytes 1179656 | tf_op jit(solution)/shard_map/ppermute | solution.py:277
  108.0 20.5 %collective-permute-start.27 = (bf16[32,6144]{1,0:T(8,128)(2,1)S(1)}, bf16[32,6144]{1,0:T(8,128)(2,1)S(1)}, u32[]{:S(2)}, u32[]{:S(2)}) collective-permute-start(bf16[32,6144]{1,0:T(8,128)(2,1)S(1)} %get-tuple-element.64), channel_id=1, source_target_pairs={{0,8},{1,9},{2,10},{3,11},{4,12},{5,13},{6,14},{7,15},{8,16},{9,17... | collective-permute-start | bytes 1179656 | tf_op jit(solution)/shard_map/ppermute | solution.py:277
  108.1 21.6 %collective-permute-start.28 = (bf16[32,6144]{1,0:T(8,128)(2,1)S(1)}, bf16[32,6144]{1,0:T(8,128)(2,1)S(1)}, u32[]{:S(2)}, u32[]{:S(2)}) collective-permute-start(bf16[32,6144]{1,0:T(8,128)(2,1)S(1)} %get-tuple-element.63), channel_id=1, source_target_pairs={{0,9},{1,8},{2,11},{3,10},{4,13},{5,12},{6,15},{7,14},{8,17},{9,16... | collective-permute-start | bytes 1179656 | tf_op jit(solution)/shard_map/ppermute | solution.py:277
  118.2 21.5 %collective-permute-start.31 = (bf16[32,6144]{1,0:T(8,128)(2,1)S(1)}, bf16[32,6144]{1,0:T(8,128)(2,1)S(1)}, u32[]{:S(2)}, u32[]{:S(2)}) collective-permute-start(bf16[32,6144]{1,0:T(8,128)(2,1)S(1)} %add_convert_fusion.2), channel_id=1, source_target_pairs={{0,11},{1,10},{2,9},{3,8},{4,15},{5,14},{6,13},{7,12},{8,19},{9,18... | collective-permute-start | bytes 1179656 | tf_op jit(solution)/shard_map/ppermute | solution.py:277
  (9 other events, 47.0 us)
